TPU v7x, 128 devices: a whole 4x4x4 slice. The times are simulated.
128 devices in a mesh: elec: 8 (over y, x_hi), slab: 16 (over x_lo, z, core).
Axes of the slice: x: 4 (x_hi: 2, x_lo: 2; x = x_hi * 2 + x_lo), y: 4, z: 4, core: 2. Of those that a mesh axis runs over, the one named last changes fastest.
Arguments:
- secondary: bfloat16 [256, 64, 64, 128], P('elec', None, 'slab'), may hold values from -3 to 3
- conductivity: float32 [64, 64, 128], P('elec', 'slab'), may hold values from 0.1 to 10
- positions: int32 [3, 256], P(None, 'elec'), may hold values from 0 to 127, as said below
- pairs: int32 [32768, 2], replicated, may hold values from 0 to 255
- weights: float32 [32768], replicated, may hold values from -0.015625 to 0.015625
Outputs:
- sensitivity: float32 [64, 64, 128], P('elec', 'slab')
Inputs may be any that keep to these rules, and one draw needn't show every extreme that they name: `positions`: row 0 is below 64, row 1 below 64, row 2 below 128.
All inputs are finite; a program needn't handle non-finite values.
Results may differ from a plain program's by a relative error of at most 0.018.
Values may be sent and summed in bfloat16 or wider, within the bound.
No kernel may reach another device: no remote copies, remote signals or barrier semaphores. Data moves between devices by JAX's collectives and lax.ppermute only.
A program may use at most 320 MiB of HBM per device.

v0:
```python
import math

import jax
import jax.numpy as jnp
from jax import lax
from jax.sharding import PartitionSpec as P


def shifted(value, axis, steps):
    count = lax.axis_size(axis)
    first, last = (max(0, -steps), min(count, count - steps))
    return lax.ppermute(value, axis, [(source, source + steps) for source in range(first, last)])


def own_pair_rows(pairs, weights, first, rows, count):
    total_pairs = pairs.shape[0]
    block = math.gcd(total_pairs, 4096)
    pair_blocks = pairs.reshape(total_pairs // block, block, 2)
    weight_blocks = weights.reshape(total_pairs // block, block)
    row_ids = jnp.arange(rows, dtype=jnp.int32) + first
    col_ids = jnp.arange(count, dtype=jnp.int32)

    def add_block(carry, item):
        pair_part, weight_part = item
        source_hot = jnp.where(
            pair_part[:, 0][:, None] == row_ids[None, :], weight_part[:, None], jnp.float32(0.0)
        )
        target_hot = (pair_part[:, 1][:, None] == col_ids[None, :]).astype(jnp.float32)
        product = lax.dot_general(
            source_hot,
            target_hot,
            (((0,), (0,)), ((), ())),
            precision=lax.Precision.HIGHEST,
            preferred_element_type=jnp.float32,
        )
        return (carry + product, None)

    start = jnp.zeros((rows, count), jnp.float32)
    summed, _ = lax.scan(add_block, start, (pair_blocks, weight_blocks))
    return summed.astype(jnp.bfloat16)


def potential(secondary, positions, z_first):
    places = positions.astype(jnp.float32)
    x_coord = jnp.arange(secondary.shape[1], dtype=jnp.int32).astype(jnp.float32)
    z_coord = (jnp.arange(secondary.shape[2], dtype=jnp.int32) + z_first).astype(jnp.float32)
    y_coord = jnp.arange(secondary.shape[3], dtype=jnp.int32).astype(jnp.float32)
    x_gap = x_coord[None, :] - places[0][:, None]
    z_gap = z_coord[None, :] - places[1][:, None]
    y_gap = y_coord[None, :] - places[2][:, None]
    dist_sq = (
        (x_gap * x_gap)[:, :, None, None]
        + (z_gap * z_gap)[:, None, :, None]
        + (y_gap * y_gap)[:, None, None, :]
    )
    return (secondary.astype(jnp.float32) + 4.0 * lax.rsqrt(dist_sq + 0.5)).astype(jnp.bfloat16)


def slopes(block):
    center = block[:, :-1, :-1]
    slope_x = block[:, 1:, :-1] - center
    slope_z = block[:, :-1, 1:] - center
    slope_y = jnp.concatenate([center[..., 1:], jnp.zeros_like(center[..., :1])], axis=-1) - center
    return (
        slope_x.astype(jnp.bfloat16),
        slope_z.astype(jnp.bfloat16),
        slope_y.astype(jnp.bfloat16),
    )


def close_rows(block):
    return jnp.concatenate([block, jnp.zeros_like(block[:, :1])], axis=1).astype(jnp.float32)


def contract(left_slopes, matrix, right_slopes):
    count = left_slopes[0].shape[0]
    total = jnp.zeros(left_slopes[0].shape[1:], jnp.float32)
    for index in range(3):
        right_flat = right_slopes[index].reshape(right_slopes[index].shape[0], -1)
        mixed = jnp.dot(matrix, right_flat, preferred_element_type=jnp.float32)
        left_flat = left_slopes[index].reshape(count, -1)
        total = total + jnp.sum(left_flat * mixed, axis=0).reshape(total.shape)
    return total


def body(secondary, conductivity, positions, pairs, weights):
    e_loc = secondary.shape[0]
    e_all = e_loc * lax.axis_size("elec")
    z_first = lax.axis_index("slab") * secondary.shape[2]
    fields = potential(secondary, positions, z_first)
    lower_plane = shifted(fields[:, :, :1], "slab", -1)
    extended = jnp.concatenate([fields, lower_plane], axis=2)
    own_rows = own_pair_rows(pairs, weights, lax.axis_index("elec") * e_loc, e_loc, e_all)
    own_slopes = slopes(close_rows(extended))
    piece_slopes = slopes(close_rows(lax.all_gather(extended, "elec", axis=0, tiled=True)))
    partial_sum = contract(own_slopes, own_rows, piece_slopes)
    summed = lax.psum_scatter(
        partial_sum.astype(jnp.bfloat16), "elec", scatter_dimension=0, tiled=True
    ).astype(jnp.float32)
    return conductivity * summed


def solution(mesh):
    return jax.shard_map(
        body,
        mesh=mesh,
        in_specs=(
            P("elec", None, "slab", None),
            P("elec", "slab", None),
            P(None, "elec"),
            P(),
            P(),
        ),
        out_specs=P("elec", "slab", None),
        check_vma=False,
    )
```

profile of v0, /device:TPU:1, one launch (start us, length us, event | category | flops | bytes accessed | tf_op | source)
XLA Modules:
  0.0 505.4 jit_solution(7519297095214013668)
XLA Ops:
  7.7 3.2 add_convert_fusion
  10.9 3.5 collective-permute-start
  14.4 8.5 %collective-permute-done = bf16[32,64,1,128]{3,1,2,0:T(8,128)(2,1)S(1)} collective-permute-done((bf16[32,64,1,128]{3,1,2,0:T(8,128)(2,1)S(1)}, bf16[32,64,1,128]{3,1,2,0:T(8,128)(2,1)S(1)}, u32[]{:S(2)}, u32[]{:S(2)}) %collective-permute-start) | collective-permute-done | bytes 524320 | tf_op jit(solution)/shard_map/ppermute | solution.py:12
  22.8 1.7 pad_maximum_fusion
  24.6 20.2 %while.11 = (s32[]{:T(128)}, f32[32,256]{1,0:T(8,128)S(1)}, s32[8,4096,2]{1,2,0:T(2,128)}, f32[8,4096]{1,0:T(8,128)S(1)}, s32[]{:T(128)}, /*index=5*/s32[]{:T(128)}, s32[]{:T(128)}) while((s32[]{:T(128)}, f32[32,256]{1,0:T(8,128)S(1)}, s32[8,4096,2]{1,2,0:T(2,128)}, f32[8,4096]{1,0:T(8,128)S(1)}, s32[]{:T(128)}, ...), condition=%wide.region_1.2_spmd.clone, body=%wide.region_0.1_spmd.clone.sunk | while | flops 403980320 | bytes 278883 | solution.py:39
  25.6 1.6 fusion.36
  40.7 1.6 fusion.36
  43.2 1.6 fusion.36
  46.5 4.5 fusion.20
  50.9 5.5 %copy.24 = f32[32,64,4,128]{3,2,1,0:T(4,128)} copy(f32[32,64,4,128]{3,1,2,0:T(8,128)S(1)} %get-tuple-element.76) | data formatting | bytes 8388608 | tf_op jit(solution)/shard_map/convert_element_type | solution.py:82
  56.5 5.7 %reshape.148 = f32[32,32768]{1,0:T(8,128)} reshape(f32[32,64,4,128]{3,2,1,0:T(4,128)} %copy.24) | data formatting | bytes 8388608 | tf_op jit(solution)/shard_map/convert_element_type | solution.py:82
  62.1 7.7 %copy.22 = f32[32,64,4,128]{3,2,1,0:T(4,128)} copy(f32[32,64,4,128]{3,1,2,0:T(8,128)} %get-tuple-element.78) | data formatting | bytes 8388608 | tf_op jit(solution)/shard_map/convert_element_type | solution.py:82
  69.9 5.6 %reshape.147 = f32[32,32768]{1,0:T(8,128)} reshape(f32[32,64,4,128]{3,2,1,0:T(4,128)} %copy.22) | data formatting | bytes 8388608 | tf_op jit(solution)/shard_map/convert_element_type | solution.py:82
  75.5 7.7 %copy.25 = f32[32,64,4,128]{3,2,1,0:T(4,128)} copy(f32[32,64,4,128]{3,1,2,0:T(8,128)} %get-tuple-element.77) | data formatting | bytes 8388608 | tf_op jit(solution)/shard_map/convert_element_type | solution.py:82
  83.2 5.7 %reshape.149 = f32[32,32768]{1,0:T(8,128)} reshape(f32[32,64,4,128]{3,2,1,0:T(4,128)} %copy.25) | data formatting | bytes 8388608 | tf_op jit(solution)/shard_map/convert_element_type | solution.py:82
  88.9 159.4 %all-gather.2.cloned.1.call-done = bf16[256,64,5,128]{3,1,2,0:T(8,128)(2,1)} async-done(((bf16[32,64,5,128]{3,1,2,0:T(8,128)(2,1)}), bf16[256,64,5,128]{3,1,2,0:T(8,128)(2,1)}) %all-gather.2.cloned.1.call-update) | async-done | bytes 20971536 | tf_op jit(solution)/shard_map/all_gather | solution.py:95
  248.3 30.2 %copy.23 = bf16[256,64,5,128]{0,3,2,1:T(8,128)(2,1)} copy(bf16[256,64,5,128]{3,1,2,0:T(8,128)(2,1)} %all-gather.2.cloned.1.call-done) | data formatting | bytes 41943040 | tf_op jit(solution)/shard_map/all_gather | solution.py:95
  278.5 23.5 %pad_convert_fusion = f32[256,65,5,128]{0,3,2,1:T(8,128)} fusion(bf16[256,64,5,128]{0,3,2,1:T(8,128)(2,1)} %copy.23), kind=kLoop, calls=%fused_computation.24 | loop fusion | flops 10649600 | bytes 63569920 | tf_op jit(solution)/shard_map/convert_element_type | solution.py:72
  302.0 22.7 %slice.68 = f32[256,64,4,127]{0,3,2,1:T(8,128)} slice(f32[256,65,5,128]{0,3,2,1:T(8,128)} %pad_convert_fusion), slice={[0:256], [0:64], [0:4], [1:128]} | slice | bytes 66584576 | tf_op jit(solution)/shard_map/slice | solution.py:63
  324.7 59.7 %fusion.14 = (bf16[256,64,4,128]{0,3,2,1:T(8,128)(2,1)}, bf16[256,64,4,128]{0,3,2,1:T(8,128)(2,1)}, bf16[256,64,4,128]{0,3,2,1:T(8,128)(2,1)}) fusion(f32[256,65,5,128]{0,3,2,1:T(8,128)} %pad_convert_fusion, f32[256,64,4,127]{0,3,2,1:T(8,128)} %slice.68), kind=kLoop, calls=%fused_computation.20 | loop fusion | flops 50331648 | bytes 184287232 | tf_op jit(solution)/shard_map/convert_element_type | solution.py:66
  384.5 11.9 %fusion.22 = f32[32768]{0:T(1024)S(1)} fusion(f32[32,32768]{1,0:T(8,128)} %reshape.148, bf16[256,32768]{0,1:T(8,128)(2,1)} %bitcast.30, f32[32,256]{1,0:T(8,128)S(1)} %get-tuple-element.37), kind=kOutput, calls=%fused_computation.37 | convolution fusion | flops 538943488 | bytes 21135360 | tf_op jit(solution)/shard_map/dot_general | solution.py:80
  396.4 11.9 %fusion.21 = f32[32768]{0:T(1024)S(1)} fusion(f32[32,32768]{1,0:T(8,128)} %reshape.147, bf16[256,32768]{0,1:T(8,128)(2,1)} %bitcast.29, f32[32,256]{1,0:T(8,128)S(1)} %get-tuple-element.37), kind=kOutput, calls=%fused_computation.36 | convolution fusion | flops 538943488 | bytes 21135360 | tf_op jit(solution)/shard_map/dot_general | solution.py:80
  408.4 11.9 %fusion.23 = f32[32768]{0:T(1024)S(1)} fusion(f32[32,32768]{1,0:T(8,128)} %reshape.149, bf16[256,32768]{0,1:T(8,128)(2,1)} %bitcast.28, f32[32,256]{1,0:T(8,128)S(1)} %get-tuple-element.37), kind=kOutput, calls=%fused_computation.38 | convolution fusion | flops 538943488 | bytes 21135360 | tf_op jit(solution)/shard_map/dot_general | solution.py:80
  422.3 75.0 %all-reduce.7.cloned.1.call-done = bf16[64,4,128]{2,1,0:T(4,128)(2,1)} async-done(((bf16[64,4,128]{2,1,0:T(4,128)(2,1)}), bf16[64,4,128]{2,1,0:T(4,128)(2,1)}) %all-reduce.7.cloned.1.call-update) | async-done | bytes 65552
  (67 shorter events, 20.3 us)
Async XLA Ops:
  6.5 241.8 %all-gather.2.cloned.1.call-start = ((), (), s32[]{:S(2)}) async-start(), calls=%async_computation | async-start | bytes 23592960 | tf_op jit(solution)/shard_map/all_gather | solution.py:95
  10.9 13.7 %copy-start.1 = (f32[32768]{0:T(1024)S(1)}, f32[32768]{0:T(1024)}, u32[]{:S(2)}) copy-start(f32[32768]{0:T(1024)} %param.11) | copy-start | bytes 393220
  10.9 11.9 %collective-permute-start = (bf16[32,64,1,128]{3,1,2,0:T(8,128)(2,1)S(1)}, bf16[32,64,1,128]{3,1,2,0:T(8,128)(2,1)S(1)}, u32[]{:S(2)}, u32[]{:S(2)}) collective-permute-start(bf16[32,64,1,128]{3,1,2,0:T(8,128)(2,1)S(1)} %slice.60), channel_id=1, source_target_pairs={{1,0},{2,1},{3,2},{4,3},{5,4},{6,5},{7,6},{8,7},{9,8},{10,9},{11,1... | collective-permute-start | bytes 1572872 | tf_op jit(solution)/shard_map/ppermute | solution.py:12
  24.5 20.3 %copy-start = (bf16[32,64,5,128]{3,1,2,0:T(8,128)(2,1)S(1)}, bf16[32,64,5,128]{3,1,2,0:T(8,128)(2,1)}, u32[]{:S(2)}) copy-start(bf16[32,64,5,128]{3,1,2,0:T(8,128)(2,1)} %pad_maximum_fusion) | copy-start | bytes 7864324
  24.5 472.7 %all-reduce.7.cloned.1.call-start = ((), (), s32[]{:S(2)}) async-start(), calls=%async_computation.1 | async-start | bytes 131072
  408.4 12.7 %copy-start.3 = (u32[128]{0:T(128)S(1)}, u32[128]{0:T(128)}, u32[]{:S(2)}) copy-start(u32[128]{0:T(128)} %constant.50) | copy-start | bytes 1540
  408.4 88.9 %copy-start.2 = (f32[8,4,128]{2,1,0:T(4,128)S(1)}, f32[8,4,128]{2,1,0:T(4,128)}, u32[]{:S(2)}) copy-start(f32[8,4,128]{2,1,0:T(4,128)} %param.8) | copy-start | bytes 49156
Sparse Core Ops, SparseCore 0:
  24.7 223.6 all-gather.1
  421.1 76.0 all-reduce.6
where the time goes:
time: 512 us; the launch traced here: 505 us
  waiting for transfers between devices  243 us (47%)
  local copies, waits for them, and re-layouts  99.5 us (19%)
  other arithmetic  96 us (19%)
  matrix products  48.9 us (10%)
  between operations  14.2 us (3%)
    all_gather x1, waiting for transfers between devices, body(): lax.all_gather(extended, 'elec', axis=0, tiled=True)  159 us
    unnamed x3, waiting for transfers between devices  75 us
    convert_element_type x1, other arithmetic, slopes(): slope_z.astype(jnp.bfloat16)  59.7 us
    convert_element_type x6, local copies, waits for them, and re-layouts, contract(): total = total + jnp.sum(left_flat * mixed, axis=0).reshape(total.shape)  38 us
    dot_general x3, matrix products, contract(): mixed = jnp.dot(matrix, right_flat, preferred_element_type=jnp.float32)  35.8 us
    all_gather x1, local copies, waits for them, and re-layouts, body(): lax.all_gather(extended, 'elec', axis=0, tiled=True)  30.2 us
    convert_element_type x2, other arithmetic, close_rows(): jnp.concatenate([block, jnp.zeros_like(block[:, :1])], axis=1)  23.9 us
    slice x2, local copies, waits for them, and re-layouts, slopes(): center[..., 1:]  23.9 us
  transfers between devices with their start and end apart: 3, of which 3 were waited for; matrix products, arithmetic and copies ran while one was open for 13% of the time, Pallas kernels for 0%

commit v1 on v0

v1 whole, which is shorter than its diff:
```python
import functools

import jax
import jax.numpy as jnp
from jax import lax
from jax.experimental import pallas as pl
from jax.experimental.pallas import tpu as pltpu
from jax.sharding import PartitionSpec as P

VMEM = 40 * 1024 * 1024
PAIR_STEP = 2048


def column(row):
    count = row.shape[1]
    own = lax.broadcasted_iota(jnp.int32, (count, count), 0) == lax.broadcasted_iota(jnp.int32, (count, count), 1)
    return jnp.sum(jnp.where(own, jnp.broadcast_to(row, (count, count)), 0.0), axis=1, keepdims=True)


def fields_kernel(nz, z_first_ref, positions_ref, block_ref, above_ref, out_ref):
    target = pl.program_id(0)
    places = positions_ref[...].astype(jnp.float32)
    x_place, z_place, y_place = (column(places[axis : axis + 1]) for axis in range(3))
    count, width = block_ref.shape[0], block_ref.shape[2]
    planes = block_ref.shape[1] // nz
    y_gap = lax.broadcasted_iota(jnp.int32, (count, width), 1).astype(jnp.float32) - y_place
    y_part = y_gap * y_gap + 0.5
    z_parts = []
    for z in range(nz):
        z_gap = (z_first_ref[0] + z).astype(jnp.float32) - z_place
        z_parts.append(z_gap * z_gap + y_part)

    def plane_pair(source_ref, row, x_first, keep):
        pair = source_ref[:, row : row + 2 * nz, :].astype(jnp.float32)
        turned = jnp.swapaxes(pair, 0, 1)
        for step in range(keep):
            x_gap = (x_first + step).astype(jnp.float32) - x_place
            x_part = x_gap * x_gap
            for z in range(nz):
                value = turned[step * nz + z] + 4.0 * lax.rsqrt(z_parts[z] + x_part)
                yield step, z, value.astype(jnp.bfloat16)

    for first in range(0, planes, 2):
        for step, z, value in plane_pair(block_ref, first * nz, target * planes + first, 2):
            out_ref[0, first + step, z] = value
    last = target == pl.num_programs(0) - 1
    for _, z, value in plane_pair(above_ref, 0, target * planes + planes, 1):
        out_ref[0, planes, z] = jnp.where(last, jnp.zeros_like(value), value)


def spread_fields(secondary, positions, z_first, groups):
    count, nx, nz, ny = secondary.shape
    planes = nx // groups
    rows = secondary.reshape(count, nx * nz, ny)
    halo_rows = 16
    return pl.pallas_call(
        functools.partial(fields_kernel, nz),
        grid=(groups,),
        in_specs=[
            pl.BlockSpec(memory_space=pltpu.SMEM),
            pl.BlockSpec(positions.shape, lambda i: (0, 0)),
            pl.BlockSpec((count, planes * nz, ny), lambda i: (0, i, 0)),
            pl.BlockSpec(
                (count, halo_rows, ny),
                lambda i: (0, jnp.minimum(i + 1, groups - 1) * (planes * nz // halo_rows), 0),
            ),
        ],
        out_specs=pl.BlockSpec((1, planes + 1, nz, count, ny), lambda i: (i, 0, 0, 0, 0)),
        out_shape=jax.ShapeDtypeStruct((groups, planes + 1, nz, count, ny), jnp.bfloat16),
        compiler_params=pltpu.CompilerParams(vmem_limit_bytes=VMEM),
        name="fields",
    )(z_first, positions, rows, rows)


def pairs_kernel(count, pairs_ref, weights_ref, out_ref, total_ref):
    total_ref[...] = jnp.zeros_like(total_ref)
    ids = lax.broadcasted_iota(jnp.int32, (count, PAIR_STEP), 0)

    @pl.loop(0, pairs_ref.shape[1] // PAIR_STEP)
    def _(step):
        part = pl.ds(pl.multiple_of(step * PAIR_STEP, PAIR_STEP), PAIR_STEP)
        weight = weights_ref[:, part]
        high = weight.astype(jnp.bfloat16).astype(jnp.float32)
        rest = weight - high
        middle = rest.astype(jnp.bfloat16).astype(jnp.float32)
        low = rest - middle
        source = ids == pairs_ref[0:1, part]
        target = jnp.where(ids == pairs_ref[1:2, part], 1.0, 0.0).astype(jnp.bfloat16)
        for term in (high, middle, low):
            hot = jnp.where(source, term, 0.0).astype(jnp.bfloat16)
            total_ref[...] += lax.dot_general(
                hot, target, (((1,), (1,)), ((), ())), preferred_element_type=jnp.float32
            )

    out_ref[...] = total_ref[...].astype(jnp.bfloat16)


def pair_matrix(pairs, weights, count):
    return pl.pallas_call(
        functools.partial(pairs_kernel, count),
        out_shape=jax.ShapeDtypeStruct((count, count), jnp.bfloat16),
        scratch_shapes=[pltpu.VMEM((count, count), jnp.float32)],
        compiler_params=pltpu.CompilerParams(vmem_limit_bytes=VMEM),
        cost_estimate=pl.CostEstimate(
            flops=6 * pairs.shape[0] * count * count, bytes_accessed=12 * pairs.shape[0], transcendentals=0
        ),
        name="pair_weights",
    )(pairs.T, weights.reshape(1, -1))


def form(matrix, slopes):
    total = None
    for slope in slopes:
        mixed = jnp.dot(matrix, slope, preferred_element_type=jnp.float32)
        term = slope.astype(jnp.float32) * mixed
        total = term if total is None else total + term
    return jnp.sum(total, axis=0)


def inner_kernel(fields_ref, matrix_ref, out_ref):
    groups, planes, nz, part, ny = fields_ref.shape
    count = groups * part
    matrix = matrix_ref[...]

    def field(x, z):
        return fields_ref[:, x, z].reshape(count, ny)

    @pl.loop(0, planes - 1)
    def _(x):
        for z in range(nz):
            here = field(x, z)
            ahead = jnp.concatenate([here[:, 1:], jnp.zeros((count, 1), here.dtype)], axis=1)
            slopes = [field(x + 1, z) - here, ahead - here]
            if z < nz - 1:
                slopes.append(field(x, z + 1) - here)
            out_ref[x, z] = form(matrix, slopes)


def outer_kernel(fields_ref, above_ref, matrix_ref, inner_ref, conductivity_ref, out_ref):
    groups, planes, part, ny = above_ref.shape
    count = groups * part
    top = inner_ref.shape[1] - 1
    matrix = matrix_ref[...]
    for x in range(planes):
        slope = above_ref[:, x].reshape(count, ny) - fields_ref[:, x].reshape(count, ny)
        rise = form(matrix, [slope])
        for z in range(top):
            out_ref[x, z] = conductivity_ref[x, z] * inner_ref[x, z]
        out_ref[x, top] = conductivity_ref[x, top] * (inner_ref[x, top] + rise)


def body(secondary, conductivity, positions, pairs, weights):
    groups = lax.axis_size("elec")
    slabs = lax.axis_size("slab")
    nz = secondary.shape[2]
    count = secondary.shape[0] * groups
    z_first = (lax.axis_index("slab") * nz).reshape(1)
    sent = spread_fields(secondary, positions, z_first, groups)
    fields = lax.all_to_all(sent, "elec", split_axis=0, concat_axis=0, tiled=True)
    matrix = pair_matrix(pairs, weights, count)
    planes = fields.shape[1] - 1
    above = lax.ppermute(fields[:, :planes, 0], "slab", [(i + 1, i) for i in range(slabs - 1)])
    params = pltpu.CompilerParams(vmem_limit_bytes=VMEM)
    inner = pl.pallas_call(
        inner_kernel,
        out_shape=jax.ShapeDtypeStruct(conductivity.shape, jnp.float32),
        compiler_params=params,
        cost_estimate=pl.CostEstimate(flops=1600000000, bytes_accessed=3000000, transcendentals=0),
        name="inner_slopes",
    )(fields, matrix)
    return pl.pallas_call(
        outer_kernel,
        out_shape=jax.ShapeDtypeStruct(conductivity.shape, jnp.float32),
        compiler_params=params,
        name="outer_slopes",
    )(fields[:, :planes, nz - 1], above, matrix, inner, conductivity)


def solution(mesh):
    return jax.shard_map(
        body,
        mesh=mesh,
        in_specs=(
            P("elec", None, "slab", None),
            P("elec", "slab", None),
            P(None, "elec"),
            P(),
            P(),
        ),
        out_specs=P("elec", "slab", None),
        check_vma=False,
    )
```

time: 512 us -> 72.1 us (0.14); the launches traced: 505 us -> 71.1 us
  waiting for transfers between devices: 243 us -> 0.01 us
  other arithmetic: 96 us -> 0 us
  local copies, waits for them, and re-layouts: 99.5 us -> 3.58 us
  matrix products: 48.9 us -> 0 us
  blocking collectives: 0 us -> 37.7 us
  Pallas kernels: 0 us -> 25.9 us
  between operations: 14.2 us -> 0.11 us
    all_gather x1 -> x0, waiting for transfers between devices: 159 us -> none  [body(): lax.all_gather(extended, 'elec', axis=0, tiled=True)]
    convert_element_type x10 -> x0, other arithmetic: 92.6 us -> none  [the longest x1 59.7 us: slopes(): slope_z.astype(jnp.bfloat16)]
    unnamed x3 -> x0, waiting for transfers between devices: 75 us -> none
    dot_general x11 -> x0, matrix products: 48.9 us -> none  [the longest x3 35.8 us: contract(): mixed = jnp.dot(matrix, right_flat, preferred_element_type=jnp.float32)]
    convert_element_type x6 -> x0, local copies, waits for them, and re-layouts: 38 us -> none  [contract(): total = total + jnp.sum(left_flat * mixed, axis=0).reshape(total.shape)]
    all_to_all x0 -> x1, blocking collectives: none -> 37.7 us  [body(): lax.all_to_all(sent, 'elec', split_axis=0, concat_axis=0, tiled=True)]
    all_gather x1 -> x0, local copies, waits for them, and re-layouts: 30.2 us -> none  [body(): lax.all_gather(extended, 'elec', axis=0, tiled=True)]
    pallas_call x0 -> x4, Pallas kernels: none -> 25.9 us  [the longest x1 17.7 us: pair_matrix(): pl.pallas_call(functools.partial(pairs_kernel, count), out_shape=jax.Shap...]
  transfers between devices with their start and end apart: 3 -> 1, of which waited for: 3 -> 0; matrix products, arithmetic and copies ran while one was open for 13% -> 1% of each run, Pallas kernels for 0% -> 31%
where the time goes in v1:
time: 72.1 us; the launch traced here: 71.1 us
  blocking collectives  37.7 us (52%)
  Pallas kernels  25.9 us (36%)
  starting transfers between devices  3.77 us (5%)
  local copies, waits for them, and re-layouts  3.58 us (5%)
    all_to_all x1, blocking collectives, body(): lax.all_to_all(sent, 'elec', split_axis=0, concat_axis=0, tiled=True)  37.7 us
    pallas_call x1, Pallas kernels, pair_matrix(): pl.pallas_call(functools.partial(pairs_kernel, count), out_shape=jax.Shap...  17.7 us
    pallas_call x1, Pallas kernels, body(): pl.pallas_call(inner_kernel, out_shape=jax.ShapeDtypeStruct(conductivity....  4.57 us
    ppermute x1, starting transfers between devices, body(): lax.ppermute(fields[:, :planes, 0], 'slab', [(i + 1, i) for i in range(sl...  3.77 us
    pallas_call x1, Pallas kernels, spread_fields(): pl.pallas_call(functools.partial(fields_kernel, nz), grid=(groups,), in_s...  2.57 us
    unnamed x10, local copies, waits for them, and re-layouts  2.29 us
  transfers between devices with their start and end apart: 1, of which 0 were waited for; matrix products, arithmetic and copies ran while one was open for 1% of the time, Pallas kernels for 31%

profile of v1, /device:TPU:1, one launch (start us, length us, event | category | flops | bytes accessed | tf_op | source)
XLA Modules:
  0.0 71.1 jit_solution(2734042430961309014)
XLA Ops:
  0.0 0.0 copy-start
  0.0 1.6 %copy-done = bf16[32,64,4,128]{3,2,1,0:T(4,128)(2,1)S(1)} copy-done((bf16[32,64,4,128]{3,2,1,0:T(4,128)(2,1)S(1)}, bf16[32,64,4,128]{3,2,1,0:T(4,128)(2,1)}, u32[]{:S(2)}) %copy-start) | copy-done | bytes 2097176
  1.6 0.0 copy-start.2
  1.6 0.7 copy-done.2
  2.3 2.6 %fields.1 = bf16[8,9,4,32,128]{4,3,2,1,0:T(8,128)(2,1)S(1)} custom-call(s32[1]{0:T(128)} %bitcast.z_first_ref, s32[3,32]{1,0:T(4,128)S(1)} %copy-done.2, bf16[32,256,128]{2,1,0:T(8,128)(2,1)S(1)} %bitcast.12, bf16[32,256,128]{2,1,0:T(8,128)(2,1)S(1)} %bitcast.13), custom_call_target="tpu_custom_call" | custom-call | tf_op jit(solution)/shard_map/fields/pallas_call | solution.py:56
  4.8 0.5 copy.8
  5.3 0.0 copy-start.3
  5.3 0.0 copy-start.4
  5.3 37.7 %all_to_all.5 = bf16[8,9,4,32,128]{4,3,1,2,0:T(8,128)(2,1)S(1)} all-to-all(bf16[8,9,4,32,128]{4,3,1,2,0:T(8,128)(2,1)S(1)} %copy.8), channel_id=1, replica_groups=mesh['elec'=8,'slab'=16] {'elec'}, dimensions={0} | all-to-all | bytes 4718592 | tf_op jit(solution)/shard_map/all_to_all | solution.py:159
  43.1 0.1 slice_bitcast_fusion
  43.2 3.8 %collective-permute-start = (bf16[8,8,32,128]{3,2,1,0:T(8,128)(2,1)S(1)}, bf16[8,8,32,128]{3,2,1,0:T(8,128)(2,1)S(1)}, u32[]{:S(2)}, u32[]{:S(2)}) collective-permute-start(bf16[8,8,32,128]{3,2,1,0:T(8,128)(2,1)S(1)} %get-tuple-element.5), channel_id=1, source_target_pairs={{1,0},{2,1},{3,2},{4,3},{5,4},{6,5},{7,6},{8,7},{9,8},{10,9},{11,1... | collective-permute-start | bytes 1572872 | tf_op jit(solution)/shard_map/ppermute | solution.py:162
  47.0 0.0 copy-done.3
  47.0 0.0 copy-done.4
  47.0 17.7 %pair_weights.1.matrix_ref = bf16[256,256]{1,0:T(8,128)(2,1)S(1)} custom-call(s32[2,32768]{1,0:T(2,128)S(1)} %bitcast.14, f32[1,32768]{1,0:T(1,128)S(1)} %bitcast.15), custom_call_target="tpu_custom_call" | custom-call | flops 12884901888 | bytes 393216 | tf_op jit(solution)/shard_map/pair_weights/pallas_call | solution.py:99
  64.7 0.7 copy.11.fields_ref
  65.4 0.0 copy-start.1
  65.4 4.6 %inner_slopes.1.inner_ref = f32[8,4,128]{2,1,0:T(4,128)S(1)} custom-call(bf16[8,9,4,32,128]{4,3,2,1,0:T(8,128)(2,1)S(1)} %copy.11.fields_ref, bf16[256,256]{1,0:T(8,128)(2,1)S(1)} %pair_weights.1.matrix_ref), custom_call_target="tpu_custom_call" | custom-call | flops 1600000000 | bytes 3000000 | tf_op jit(solution)/shard_map/inner_slopes/pallas_call | solution.py:164
  70.0 0.0 collective-permute-done.above_ref
  70.0 0.0 copy-done.1
  70.0 1.1 %outer_slopes.1 = f32[8,4,128]{2,1,0:T(4,128)} custom-call(bf16[8,8,32,128]{3,2,1,0:T(8,128)(2,1)S(1)} %get-tuple-element.6.fields_ref, bf16[8,8,32,128]{3,2,1,0:T(8,128)(2,1)S(1)} %collective-permute-done.above_ref, bf16[256,256]{1,0:T(8,128)(2,1)S(1)} %pair_weights.1.matrix_ref, f32[8,4,128]{2,1,0:T(4,128)S(1)} %inner_slopes.1.inner_ref, ...), custom_call_target="tpu_custom_call" | custom-call | tf_op jit(solution)/shard_map/outer_slopes/pallas_call | solution.py:171
Async XLA Ops:
  0.0 1.6 %copy-start = (bf16[32,64,4,128]{3,2,1,0:T(4,128)(2,1)S(1)}, bf16[32,64,4,128]{3,2,1,0:T(4,128)(2,1)}, u32[]{:S(2)}) copy-start(bf16[32,64,4,128]{3,2,1,0:T(4,128)(2,1)} %param.5) | copy-start | bytes 6291460
  1.6 0.7 copy-start.2
  5.3 41.7 %copy-start.3 = (s32[32768,2]{0,1:T(2,128)S(1)}, s32[32768,2]{0,1:T(2,128)}, u32[]{:S(2)}) copy-start(s32[32768,2]{0,1:T(2,128)} %param.8) | copy-start | bytes 786436
  5.3 41.7 %copy-start.4 = (f32[32768]{0:T(1024)S(1)}, f32[32768]{0:T(1024)}, u32[]{:S(2)}) copy-start(f32[32768]{0:T(1024)} %param.9) | copy-start | bytes 393220
  43.2 26.8 %collective-permute-start = (bf16[8,8,32,128]{3,2,1,0:T(8,128)(2,1)S(1)}, bf16[8,8,32,128]{3,2,1,0:T(8,128)(2,1)S(1)}, u32[]{:S(2)}, u32[]{:S(2)}) collective-permute-start(bf16[8,8,32,128]{3,2,1,0:T(8,128)(2,1)S(1)} %get-tuple-element.5), channel_id=1, source_target_pairs={{1,0},{2,1},{3,2},{4,3},{5,4},{6,5},{7,6},{8,7},{9,8},{10,9},{11,1... | collective-permute-start | bytes 1572872 | tf_op jit(solution)/shard_map/ppermute | solution.py:162
  65.4 4.6 %copy-start.1 = (f32[8,4,128]{2,1,0:T(4,128)S(1)}, f32[8,4,128]{2,1,0:T(4,128)}, u32[]{:S(2)}) copy-start(f32[8,4,128]{2,1,0:T(4,128)} %conductivity_ref.1) | copy-start | bytes 49156

commit v2 on v1

v2 whole, which is shorter than its diff:
```python
import functools

import jax
import jax.numpy as jnp
from jax import lax
from jax.experimental import pallas as pl
from jax.experimental.pallas import tpu as pltpu
from jax.sharding import PartitionSpec as P

VMEM = 40 * 1024 * 1024
PAIR_STEP = 2048
HALO_ROWS = 16
OFFSETS = [(0, 0), (0, 1), (2, 0), (2, 1), (1, 1), (3, 0), (3, 1), (1, 0)]


def partner(me, offset, groups):
    y_step, flip = offset
    return (me // 2 + y_step) % (groups // 2) * 2 + (me % 2 + flip) % 2


def origin(me, offset, groups):
    return partner(me, ((groups // 2 - offset[0]) % (groups // 2), offset[1]), groups)


def column(row):
    count = row.shape[1]
    own = lax.broadcasted_iota(jnp.int32, (count, count), 0) == lax.broadcasted_iota(jnp.int32, (count, count), 1)
    return jnp.sum(jnp.where(own, jnp.broadcast_to(row, (count, count)), 0.0), axis=1, keepdims=True)


def fields_kernel(offsets, groups, nz, place_ref, positions_ref, rows_ref, *refs):
    outs, (block_ref, halo_ref, block_sem, halo_sem) = refs[:-4], refs[-4:]
    me, z_first = place_ref[0], place_ref[1] * nz
    count, width = rows_ref.shape[0], rows_ref.shape[2]
    total = rows_ref.shape[1]
    planes = total // nz // groups
    targets = [partner(me, offset, groups) for offset in offsets]
    copies = []
    for slot, target in enumerate(targets):
        first = pl.multiple_of(target * (planes * nz), planes * nz)
        after = pl.multiple_of(jnp.minimum(first + planes * nz, total - HALO_ROWS), HALO_ROWS)
        copies.append((
            pltpu.make_async_copy(
                rows_ref.at[:, pl.ds(first, planes * nz), :], block_ref.at[slot], block_sem.at[slot]
            ),
            pltpu.make_async_copy(
                rows_ref.at[:, pl.ds(after, HALO_ROWS), :], halo_ref.at[slot], halo_sem.at[slot]
            ),
        ))
        for copy in copies[-1]:
            copy.start()

    places = positions_ref[...].astype(jnp.float32)
    x_place, z_place, y_place = (column(places[axis : axis + 1]) for axis in range(3))
    y_gap = lax.broadcasted_iota(jnp.int32, (count, width), 1).astype(jnp.float32) - y_place
    y_part = y_gap * y_gap + 0.5
    z_parts = []
    for z in range(nz):
        z_gap = (z_first + z).astype(jnp.float32) - z_place
        z_parts.append(z_gap * z_gap + y_part)

    def planes_of(pair, x_first, keep):
        turned = jnp.swapaxes(pair.astype(jnp.float32), 0, 1)
        for step in range(keep):
            x_gap = (x_first + step).astype(jnp.float32) - x_place
            x_part = x_gap * x_gap
            for z in range(nz):
                value = turned[step * nz + z] + 4.0 * lax.rsqrt(z_parts[z] + x_part)
                yield step, z, value.astype(jnp.bfloat16)

    for slot, target in enumerate(targets):
        out_ref = outs[slot]
        copies[slot][0].wait()
        for first in range(0, planes, 2):
            pair = block_ref[slot, :, first * nz : (first + 2) * nz, :]
            for step, z, value in planes_of(pair, target * planes + first, 2):
                out_ref[z, first + step] = value
        copies[slot][1].wait()
        last = target == groups - 1
        for _, z, value in planes_of(halo_ref[slot, :, : 2 * nz, :], (target + 1) * planes, 1):
            out_ref[z, planes] = jnp.where(last, jnp.zeros_like(value), value)


def spread_fields(offsets, place, secondary, positions, groups):
    count, nx, nz, ny = secondary.shape
    planes = nx // groups
    slots = len(offsets)
    rows = secondary.reshape(count, nx * nz, ny)
    return pl.pallas_call(
        functools.partial(fields_kernel, offsets, groups, nz),
        in_specs=[
            pl.BlockSpec(memory_space=pltpu.SMEM),
            pl.BlockSpec(memory_space=pltpu.VMEM),
            pl.BlockSpec(memory_space=pl.ANY),
        ],
        out_specs=[pl.BlockSpec(memory_space=pltpu.VMEM)] * slots,
        out_shape=[jax.ShapeDtypeStruct((nz, planes + 1, count, ny), jnp.bfloat16)] * slots,
        scratch_shapes=[
            pltpu.VMEM((slots, count, planes * nz, ny), jnp.bfloat16),
            pltpu.VMEM((slots, count, HALO_ROWS, ny), jnp.bfloat16),
            pltpu.SemaphoreType.DMA((slots,)),
            pltpu.SemaphoreType.DMA((slots,)),
        ],
        compiler_params=pltpu.CompilerParams(vmem_limit_bytes=VMEM),
        name="fields",
    )(place, positions, rows)


def pairs_kernel(groups, count, place_ref, pairs_ref, weights_ref, out_ref, total_ref):
    total_ref[...] = jnp.zeros_like(total_ref)
    part = count // groups
    ids = []
    for offset in OFFSETS:
        first = origin(place_ref[0], offset, groups) * part
        ids.append(lax.broadcasted_iota(jnp.int32, (part, PAIR_STEP), 0) + first)
    ids = jnp.concatenate(ids, axis=0)

    @pl.loop(0, pairs_ref.shape[1] // PAIR_STEP)
    def _(step):
        span = pl.ds(pl.multiple_of(step * PAIR_STEP, PAIR_STEP), PAIR_STEP)
        weight = weights_ref[:, span]
        high = weight.astype(jnp.bfloat16).astype(jnp.float32)
        source = ids == pairs_ref[0:1, span]
        target = jnp.where(ids == pairs_ref[1:2, span], 1.0, 0.0).astype(jnp.bfloat16)
        for term in (high, weight - high):
            hot = jnp.where(source, term, 0.0).astype(jnp.bfloat16)
            total_ref[...] += lax.dot_general(
                hot, target, (((1,), (1,)), ((), ())), preferred_element_type=jnp.float32
            )

    out_ref[...] = total_ref[...].astype(jnp.bfloat16)


def pair_matrix(place, pairs, weights, count, groups):
    return pl.pallas_call(
        functools.partial(pairs_kernel, groups, count),
        in_specs=[
            pl.BlockSpec(memory_space=pltpu.SMEM),
            pl.BlockSpec(memory_space=pltpu.VMEM),
            pl.BlockSpec(memory_space=pltpu.VMEM),
        ],
        out_shape=jax.ShapeDtypeStruct((count, count), jnp.bfloat16),
        scratch_shapes=[pltpu.VMEM((count, count), jnp.float32)],
        compiler_params=pltpu.CompilerParams(vmem_limit_bytes=VMEM),
        cost_estimate=pl.CostEstimate(
            flops=4 * pairs.shape[0] * count * count, bytes_accessed=12 * pairs.shape[0], transcendentals=0
        ),
        name="pair_weights",
    )(place, pairs.T, weights.reshape(1, -1))


def form(matrix, slopes):
    total = None
    for slope in slopes:
        mixed = jnp.dot(matrix, slope, preferred_element_type=jnp.float32)
        term = slope.astype(jnp.float32) * mixed
        total = term if total is None else total + term
    return jnp.sum(total, axis=0)


def inner_kernel(matrix_ref, *refs):
    blocks, out_ref = refs[:-1], refs[-1]
    nz, planes, _, ny = blocks[0].shape
    matrix = matrix_ref[...]
    count = matrix.shape[0]

    def field(x, z):
        return jnp.concatenate([block[z, x] for block in blocks], axis=0)

    @pl.loop(0, planes - 1)
    def _(x):
        for z in range(nz):
            here = field(x, z)
            ahead = jnp.concatenate([here[:, 1:], jnp.zeros((count, 1), here.dtype)], axis=1)
            slopes = [field(x + 1, z) - here, ahead - here]
            if z < nz - 1:
                slopes.append(field(x, z + 1) - here)
            out_ref[x, z] = form(matrix, slopes)


def outer_kernel(matrix_ref, inner_ref, conductivity_ref, above_ref, *refs):
    blocks, out_ref = refs[:-1], refs[-1]
    planes = above_ref.shape[1]
    top = blocks[0].shape[0] - 1
    matrix = matrix_ref[...]
    for x in range(planes):
        here = jnp.concatenate([block[top, x] for block in blocks], axis=0)
        slope = above_ref[:, x].reshape(here.shape) - here
        rise = form(matrix, [slope])
        for z in range(top):
            out_ref[x, z] = conductivity_ref[x, z] * inner_ref[x, z]
        out_ref[x, top] = conductivity_ref[x, top] * (inner_ref[x, top] + rise)


def body(secondary, conductivity, positions, pairs, weights):
    groups = lax.axis_size("elec")
    slabs = lax.axis_size("slab")
    count = secondary.shape[0] * groups
    place = jnp.stack([lax.axis_index("elec"), lax.axis_index("slab")])
    blocks = spread_fields(OFFSETS, place, secondary, positions, groups)
    planes = blocks[0].shape[1] - 1
    blocks = [blocks[0]] + [
        lax.ppermute(block, "elec", [(i, partner(i, offset, groups)) for i in range(groups)])
        for block, offset in zip(blocks[1:], OFFSETS[1:])
    ]
    matrix = pair_matrix(place, pairs, weights, count, groups)
    plane = jnp.stack([block[0, :planes] for block in blocks])
    plane, matrix = lax.optimization_barrier((plane, matrix))
    above = lax.ppermute(plane, "slab", [(i + 1, i) for i in range(slabs - 1)])
    params = pltpu.CompilerParams(vmem_limit_bytes=VMEM)
    inner = pl.pallas_call(
        inner_kernel,
        out_shape=jax.ShapeDtypeStruct(conductivity.shape, jnp.float32),
        compiler_params=params,
        cost_estimate=pl.CostEstimate(flops=1600000000, bytes_accessed=3000000, transcendentals=0),
        name="inner_slopes",
    )(matrix, *blocks)
    return pl.pallas_call(
        outer_kernel,
        out_shape=jax.ShapeDtypeStruct(conductivity.shape, jnp.float32),
        compiler_params=params,
        name="outer_slopes",
    )(matrix, inner, conductivity, above, *blocks)


def solution(mesh):
    return jax.shard_map(
        body,
        mesh=mesh,
        in_specs=(
            P("elec", None, "slab", None),
            P("elec", "slab", None),
            P(None, "elec"),
            P(),
            P(),
        ),
        out_specs=P("elec", "slab", None),
        check_vma=False,
    )
```

time: 72.1 us -> 53.4 us (0.74); the launches traced: 71.1 us -> 53.2 us
  blocking collectives: 37.7 us -> 0 us
  starting transfers between devices: 3.77 us -> 18.6 us
  waiting for transfers between devices: 0.01 us -> 10.9 us
  Pallas kernels: 25.9 us -> 21.2 us
  local copies, waits for them, and re-layouts: 3.58 us -> 2.38 us
    all_to_all x1 -> x0, blocking collectives: 37.7 us -> none  [body(): lax.all_to_all(sent, 'elec', split_axis=0, concat_axis=0, tiled=True)]
    ppermute x1 -> x8, starting transfers between devices: 3.77 us -> 18.6 us  [the longest x7 13.4 us: body(): lax.ppermute(block, 'elec', [(i, partner(i, offset, groups)) for i in ran...]
    ppermute x1 -> x8, waiting for transfers between devices: 0.01 us -> 10.9 us  [the longest x7 7.21 us: body(): lax.ppermute(block, 'elec', [(i, partner(i, offset, groups)) for i in ran...]
    pallas_call x2, Pallas kernels: 20.2 us -> 15.5 us  [the longest x1 12.4 us: pair_matrix(): pl.pallas_call(functools.partial(pairs_kernel, groups, count), in_specs=[...]
    unnamed x10 -> x17, local copies, waits for them, and re-layouts: 2.29 us -> 2.37 us
  transfers between devices with their start and end apart: 1 -> 8, of which waited for: 0 -> 4; matrix products, arithmetic and copies ran while one was open for 1% -> 0% of each run, Pallas kernels for 31% -> 32%
where the time goes in v2:
time: 53.4 us; the launch traced here: 53.2 us
  Pallas kernels  21.2 us (40%)
  starting transfers between devices  18.6 us (35%)
  waiting for transfers between devices  10.9 us (20%)
  local copies, waits for them, and re-layouts  2.38 us (4%)
    ppermute x7, starting transfers between devices, body(): lax.ppermute(block, 'elec', [(i, partner(i, offset, groups)) for i in ran...  13.4 us
    pallas_call x1, Pallas kernels, pair_matrix(): pl.pallas_call(functools.partial(pairs_kernel, groups, count), in_specs=[...  12.4 us
    ppermute x7, waiting for transfers between devices, body(): lax.ppermute(block, 'elec', [(i, partner(i, offset, groups)) for i in ran...  7.21 us
    ppermute x1, starting transfers between devices, body(): above = lax.ppermute(plane, 'slab', [(i + 1, i) for i in range(slabs - 1)])  5.18 us
    pallas_call x1, Pallas kernels, body(): pl.pallas_call(inner_kernel, out_shape=jax.ShapeDtypeStruct(conductivity....  4.66 us
    ppermute x1, waiting for transfers between devices, body(): above = lax.ppermute(plane, 'slab', [(i + 1, i) for i in range(slabs - 1)])  3.71 us
    pallas_call x1, Pallas kernels, spread_fields(): pl.pallas_call(functools.partial(fields_kernel, offsets, groups, nz), in_...  3.04 us
    unnamed x17, local copies, waits for them, and re-layouts  2.37 us
  transfers between devices with their start and end apart: 8, of which 4 were waited for; matrix products, arithmetic and copies ran while one was open for 0% of the time, Pallas kernels for 32%

profile of v2, /device:TPU:1, one launch (start us, length us, event | category | flops | bytes accessed | tf_op | source)
XLA Modules:
  0.0 53.2 jit_solution(934735884158189073)
XLA Ops:
  0.0 0.1 pad_add_fusion.place_ref
  0.1 1.6 %copy-done = bf16[32,64,4,128]{3,2,1,0:T(4,128)(2,1)S(1)} copy-done((bf16[32,64,4,128]{3,2,1,0:T(4,128)(2,1)S(1)}, bf16[32,64,4,128]{3,2,1,0:T(4,128)(2,1)}, u32[]{:S(2)}) %copy-start) | copy-done | bytes 2097176
  1.7 0.7 %copy-done.2 = s32[3,32]{1,0:T(4,128)S(1)} copy-done((s32[3,32]{1,0:T(4,128)S(1)}, s32[3,32]{1,0:T(4,128)}, u32[]{:S(2)}) %copy-start.2) | copy-done | bytes 408
  2.4 3.0 %fields.1 = (bf16[4,9,32,128]{3,2,1,0:T(8,128)(2,1)S(1)}, bf16[4,9,32,128]{3,2,1,0:T(8,128)(2,1)S(1)}, bf16[4,9,32,128]{3,2,1,0:T(8,128)(2,1)S(1)}, bf16[4,9,32,...) custom-call(s32[2]{0:T(128)S(1)} %pad_add_fusion.place_ref, ...), custom_call_target="tpu_custom_call" | custom-call | tf_op jit(solution)/shard_map/fields/pallas_call | solution.py:89
  5.4 3.7 %collective-permute-start = (bf16[4,9,32,128]{3,2,1,0:T(8,128)(2,1)S(1)}, bf16[4,9,32,128]{3,2,1,0:T(8,128)(2,1)S(1)}, u32[]{:S(2)}, u32[]{:S(2)}) collective-permute-start(bf16[4,9,32,128]{3,2,1,0:T(8,128)(2,1)S(1)} %get-tuple-element.16), channel_id=1, source_target_pairs={{0,16},{16,0},{32,48},{48,32},{64,80},{80,64},{96,112},{112,96},{1... | collective-permute-start | bytes 884744 | tf_op jit(solution)/shard_map/ppermute | solution.py:203
  9.1 2.9 %collective-permute-start.1 = (bf16[4,9,32,128]{3,2,1,0:T(8,128)(2,1)S(1)}, bf16[4,9,32,128]{3,2,1,0:T(8,128)(2,1)S(1)}, u32[]{:S(2)}, u32[]{:S(2)}) collective-permute-start(bf16[4,9,32,128]{3,2,1,0:T(8,128)(2,1)S(1)} %get-tuple-element.17), channel_id=1, source_target_pairs={{0,64},{16,80},{32,96},{48,112},{64,0},{80,16},{96,32},{112,48},{1... | collective-permute-start | bytes 884744 | tf_op jit(solution)/shard_map/ppermute | solution.py:203
  12.0 0.0 collective-permute-start.2
  12.0 3.8 %collective-permute-start.3 = (bf16[4,9,32,128]{3,2,1,0:T(8,128)(2,1)S(1)}, bf16[4,9,32,128]{3,2,1,0:T(8,128)(2,1)S(1)}, u32[]{:S(2)}, u32[]{:S(2)}) collective-permute-start(bf16[4,9,32,128]{3,2,1,0:T(8,128)(2,1)S(1)} %get-tuple-element.19), channel_id=1, source_target_pairs={{0,48},{16,32},{32,80},{48,64},{64,112},{80,96},{96,16},{112,0},{1... | collective-permute-start | bytes 884744 | tf_op jit(solution)/shard_map/ppermute | solution.py:203
  15.7 1.4 %collective-permute-start.4 = (bf16[4,9,32,128]{3,2,1,0:T(8,128)(2,1)S(1)}, bf16[4,9,32,128]{3,2,1,0:T(8,128)(2,1)S(1)}, u32[]{:S(2)}, u32[]{:S(2)}) collective-permute-start(bf16[4,9,32,128]{3,2,1,0:T(8,128)(2,1)S(1)} %get-tuple-element.20), channel_id=1, source_target_pairs={{0,96},{16,112},{32,0},{48,16},{64,32},{80,48},{96,64},{112,80},{1... | collective-permute-start | bytes 884744 | tf_op jit(solution)/shard_map/ppermute | solution.py:203
  17.1 12.4 %pair_weights.1.matrix_ref = bf16[256,256]{1,0:T(8,128)(2,1)S(1)} custom-call(s32[2]{0:T(128)S(1)} %pad_add_fusion.place_ref, s32[2,32768]{1,0:T(2,128)S(1)} %bitcast.6, f32[1,32768]{1,0:T(1,128)S(1)} %bitcast.7), custom_call_target="tpu_custom_call" | custom-call | flops 8589934592 | bytes 393216 | tf_op jit(solution)/shard_map/pair_weights/pallas_call | solution.py:135
  29.6 0.0 collective-permute-done.refs_1_
  29.6 1.5 %collective-permute-start.5 = (bf16[4,9,32,128]{3,2,1,0:T(8,128)(2,1)S(1)}, bf16[4,9,32,128]{3,2,1,0:T(8,128)(2,1)S(1)}, u32[]{:S(2)}, u32[]{:S(2)}) collective-permute-start(bf16[4,9,32,128]{3,2,1,0:T(8,128)(2,1)S(1)} %get-tuple-element.21), channel_id=1, source_target_pairs={{0,112},{16,96},{32,16},{48,0},{64,48},{80,32},{96,80},{112,64},{1... | collective-permute-start | bytes 884744 | tf_op jit(solution)/shard_map/ppermute | solution.py:203
  31.1 0.0 collective-permute-done.1.refs_2_
  31.1 0.1 collective-permute-start.6
  31.3 0.0 collective-permute-done.2.refs_3_
  31.3 0.0 collective-permute-done.3.refs_4_
  31.3 0.1 collective-permute-done.4.refs_5_
  31.5 7.0 %collective-permute-done.5.refs_6_ = bf16[4,9,32,128]{3,2,1,0:T(8,128)(2,1)S(1)} collective-permute-done((bf16[4,9,32,128]{3,2,1,0:T(8,128)(2,1)S(1)}, bf16[4,9,32,128]{3,2,1,0:T(8,128)(2,1)S(1)}, u32[]{:S(2)}, u32[]{:S(2)}) %collective-permute-start.5) | collective-permute-done | bytes 294944 | tf_op jit(solution)/shard_map/ppermute | solution.py:203
  38.5 0.1 collective-permute-done.6.refs_7_
  38.6 0.0 copy-start.1
  38.6 5.2 %collective-permute-start.7 = (bf16[8,8,32,128]{3,2,1,0:T(8,128)(2,1)S(1)}, bf16[8,8,32,128]{3,2,1,0:T(8,128)(2,1)S(1)}, u32[]{:S(2)}, u32[]{:S(2)}) collective-permute-start(bf16[8,8,32,128]{3,2,1,0:T(8,128)(2,1)S(1)} %slice_dynamic-update-slice_fusion), channel_id=1, source_target_pairs={{1,0},{2,1},{3,2},{4,3},{5,4},{6,5},{7,6},{8,7},{9,8},{10,9},{11,1... | collective-permute-start | bytes 1572872 | tf_op jit(solution)/shard_map/ppermute | solution.py:209
  43.8 4.7 %inner_slopes.1.inner_ref = f32[8,4,128]{2,1,0:T(4,128)S(1)} custom-call(bf16[256,256]{1,0:T(8,128)(2,1)S(1)} %pair_weights.1.matrix_ref, bf16[4,9,32,128]{3,2,1,0:T(8,128)(2,1)S(1)} %get-tuple-element.15.refs_0_, bf16[4,9,32,128]{3,2,1,0:T(8,128)(2,1)S(1)} %collective-permute-done.refs_1_, bf16[4,9,32,128]{3,2,1,0:T(8,128)(2,1)S(1)} %collective-permute-done.1.refs_2_, ...), custom_call_target="tpu_custom_call" | custom-call | flops 1600000000 | bytes 3000000 | tf_op jit(solution)/shard_map/inner_slopes/pallas_call | solution.py:211
  48.4 3.7 %collective-permute-done.7.above_ref = bf16[8,8,32,128]{3,2,1,0:T(8,128)(2,1)S(1)} collective-permute-done((bf16[8,8,32,128]{3,2,1,0:T(8,128)(2,1)S(1)}, bf16[8,8,32,128]{3,2,1,0:T(8,128)(2,1)S(1)}, u32[]{:S(2)}, u32[]{:S(2)}) %collective-permute-start.7) | collective-permute-done | bytes 524320 | tf_op jit(solution)/shard_map/ppermute | solution.py:209
  52.2 1.1 %outer_slopes.1 = f32[8,4,128]{2,1,0:T(4,128)} custom-call(bf16[256,256]{1,0:T(8,128)(2,1)S(1)} %pair_weights.1.matrix_ref, f32[8,4,128]{2,1,0:T(4,128)S(1)} %inner_slopes.1.inner_ref, f32[8,4,128]{2,1,0:T(4,128)S(1)} %copy-done.1, bf16[8,8,32,128]{3,2,1,0:T(8,128)(2,1)S(1)} %collective-permute-done.7.above_ref, ...), custom_call_target="tpu_custom_call" | custom-call | tf_op jit(solution)/shard_map/outer_slopes/pallas_call | solution.py:218
  (15 shorter events, 0.1 us)
Async XLA Ops:
  0.1 1.6 %copy-start = (bf16[32,64,4,128]{3,2,1,0:T(4,128)(2,1)S(1)}, bf16[32,64,4,128]{3,2,1,0:T(4,128)(2,1)}, u32[]{:S(2)}) copy-start(bf16[32,64,4,128]{3,2,1,0:T(4,128)(2,1)} %param.5) | copy-start | bytes 6291460
  1.7 0.7 %copy-start.2 = (s32[3,32]{1,0:T(4,128)S(1)}, s32[3,32]{1,0:T(4,128)}, u32[]{:S(2)}) copy-start(s32[3,32]{1,0:T(4,128)} %positions_ref.1) | copy-start | bytes 1156
  2.3 14.8 %copy-start.3 = (s32[32768,2]{0,1:T(2,128)S(1)}, s32[32768,2]{0,1:T(2,128)}, u32[]{:S(2)}) copy-start(s32[32768,2]{0,1:T(2,128)} %param.8) | copy-start | bytes 786436
  2.4 14.8 %copy-start.4 = (f32[32768]{0:T(1024)S(1)}, f32[32768]{0:T(1024)}, u32[]{:S(2)}) copy-start(f32[32768]{0:T(1024)} %param.9) | copy-start | bytes 393220
  5.4 24.2 %collective-permute-start = (bf16[4,9,32,128]{3,2,1,0:T(8,128)(2,1)S(1)}, bf16[4,9,32,128]{3,2,1,0:T(8,128)(2,1)S(1)}, u32[]{:S(2)}, u32[]{:S(2)}) collective-permute-start(bf16[4,9,32,128]{3,2,1,0:T(8,128)(2,1)S(1)} %get-tuple-element.16), channel_id=1, source_target_pairs={{0,16},{16,0},{32,48},{48,32},{64,80},{80,64},{96,112},{112,96},{1... | collective-permute-start | bytes 884744 | tf_op jit(solution)/shard_map/ppermute | solution.py:203
  9.1 22.1 %collective-permute-start.1 = (bf16[4,9,32,128]{3,2,1,0:T(8,128)(2,1)S(1)}, bf16[4,9,32,128]{3,2,1,0:T(8,128)(2,1)S(1)}, u32[]{:S(2)}, u32[]{:S(2)}) collective-permute-start(bf16[4,9,32,128]{3,2,1,0:T(8,128)(2,1)S(1)} %get-tuple-element.17), channel_id=1, source_target_pairs={{0,64},{16,80},{32,96},{48,112},{64,0},{80,16},{96,32},{112,48},{1... | collective-permute-start | bytes 884744 | tf_op jit(solution)/shard_map/ppermute | solution.py:203
  12.0 19.3 %collective-permute-start.2 = (bf16[4,9,32,128]{3,2,1,0:T(8,128)(2,1)S(1)}, bf16[4,9,32,128]{3,2,1,0:T(8,128)(2,1)S(1)}, u32[]{:S(2)}, u32[]{:S(2)}) collective-permute-start(bf16[4,9,32,128]{3,2,1,0:T(8,128)(2,1)S(1)} %get-tuple-element.18), channel_id=1, source_target_pairs={{0,80},{16,64},{32,112},{48,96},{64,16},{80,0},{96,48},{112,32},{1... | collective-permute-start | bytes 884744 | tf_op jit(solution)/shard_map/ppermute | solution.py:203
  12.0 19.3 %collective-permute-start.3 = (bf16[4,9,32,128]{3,2,1,0:T(8,128)(2,1)S(1)}, bf16[4,9,32,128]{3,2,1,0:T(8,128)(2,1)S(1)}, u32[]{:S(2)}, u32[]{:S(2)}) collective-permute-start(bf16[4,9,32,128]{3,2,1,0:T(8,128)(2,1)S(1)} %get-tuple-element.19), channel_id=1, source_target_pairs={{0,48},{16,32},{32,80},{48,64},{64,112},{80,96},{96,16},{112,0},{1... | collective-permute-start | bytes 884744 | tf_op jit(solution)/shard_map/ppermute | solution.py:203
  15.7 15.7 %collective-permute-start.4 = (bf16[4,9,32,128]{3,2,1,0:T(8,128)(2,1)S(1)}, bf16[4,9,32,128]{3,2,1,0:T(8,128)(2,1)S(1)}, u32[]{:S(2)}, u32[]{:S(2)}) collective-permute-start(bf16[4,9,32,128]{3,2,1,0:T(8,128)(2,1)S(1)} %get-tuple-element.20), channel_id=1, source_target_pairs={{0,96},{16,112},{32,0},{48,16},{64,32},{80,48},{96,64},{112,80},{1... | collective-permute-start | bytes 884744 | tf_op jit(solution)/shard_map/ppermute | solution.py:203
  29.6 8.9 %collective-permute-start.5 = (bf16[4,9,32,128]{3,2,1,0:T(8,128)(2,1)S(1)}, bf16[4,9,32,128]{3,2,1,0:T(8,128)(2,1)S(1)}, u32[]{:S(2)}, u32[]{:S(2)}) collective-permute-start(bf16[4,9,32,128]{3,2,1,0:T(8,128)(2,1)S(1)} %get-tuple-element.21), channel_id=1, source_target_pairs={{0,112},{16,96},{32,16},{48,0},{64,48},{80,32},{96,80},{112,64},{1... | collective-permute-start | bytes 884744 | tf_op jit(solution)/shard_map/ppermute | solution.py:203
  31.1 7.4 %collective-permute-start.6 = (bf16[4,9,32,128]{3,2,1,0:T(8,128)(2,1)S(1)}, bf16[4,9,32,128]{3,2,1,0:T(8,128)(2,1)S(1)}, u32[]{:S(2)}, u32[]{:S(2)}) collective-permute-start(bf16[4,9,32,128]{3,2,1,0:T(8,128)(2,1)S(1)} %get-tuple-element.22), channel_id=1, source_target_pairs={{0,32},{16,48},{32,64},{48,80},{64,96},{80,112},{96,0},{112,16},{1... | collective-permute-start | bytes 884744 | tf_op jit(solution)/shard_map/ppermute | solution.py:203
  38.6 13.6 %copy-start.1 = (f32[8,4,128]{2,1,0:T(4,128)S(1)}, f32[8,4,128]{2,1,0:T(4,128)}, u32[]{:S(2)}) copy-start(f32[8,4,128]{2,1,0:T(4,128)} %conductivity_ref.1) | copy-start | bytes 49156
  38.6 13.6 %collective-permute-start.7 = (bf16[8,8,32,128]{3,2,1,0:T(8,128)(2,1)S(1)}, bf16[8,8,32,128]{3,2,1,0:T(8,128)(2,1)S(1)}, u32[]{:S(2)}, u32[]{:S(2)}) collective-permute-start(bf16[8,8,32,128]{3,2,1,0:T(8,128)(2,1)S(1)} %slice_dynamic-update-slice_fusion), channel_id=1, source_target_pairs={{1,0},{2,1},{3,2},{4,3},{5,4},{6,5},{7,6},{8,7},{9,8},{10,9},{11,1... | collective-permute-start | bytes 1572872 | tf_op jit(solution)/shard_map/ppermute | solution.py:209

commit v3 on v2

--- a/solution.py
+++ b/solution.py
@@ -10,6 +10,7 @@
 VMEM = 40 * 1024 * 1024
 PAIR_STEP = 2048
 HALO_ROWS = 16
+EARLY = 6
 OFFSETS = [(0, 0), (0, 1), (2, 0), (2, 1), (1, 1), (3, 0), (3, 1), (1, 0)]
 
 
@@ -29,26 +30,12 @@
 
 
 def fields_kernel(offsets, groups, nz, place_ref, positions_ref, rows_ref, *refs):
-    outs, (block_ref, halo_ref, block_sem, halo_sem) = refs[:-4], refs[-4:]
+    outs = refs
     me, z_first = place_ref[0], place_ref[1] * nz
     count, width = rows_ref.shape[0], rows_ref.shape[2]
     total = rows_ref.shape[1]
     planes = total // nz // groups
     targets = [partner(me, offset, groups) for offset in offsets]
-    copies = []
-    for slot, target in enumerate(targets):
-        first = pl.multiple_of(target * (planes * nz), planes * nz)
-        after = pl.multiple_of(jnp.minimum(first + planes * nz, total - HALO_ROWS), HALO_ROWS)
-        copies.append((
-            pltpu.make_async_copy(
-                rows_ref.at[:, pl.ds(first, planes * nz), :], block_ref.at[slot], block_sem.at[slot]
-            ),
-            pltpu.make_async_copy(
-                rows_ref.at[:, pl.ds(after, HALO_ROWS), :], halo_ref.at[slot], halo_sem.at[slot]
-            ),
-        ))
-        for copy in copies[-1]:
-            copy.start()
 
     places = positions_ref[...].astype(jnp.float32)
     x_place, z_place, y_place = (column(places[axis : axis + 1]) for axis in range(3))
@@ -70,14 +57,14 @@
 
     for slot, target in enumerate(targets):
         out_ref = outs[slot]
-        copies[slot][0].wait()
+        start = pl.multiple_of(target * (planes * nz), planes * nz)
+        after = pl.multiple_of(jnp.minimum(start + planes * nz, total - HALO_ROWS), HALO_ROWS)
         for first in range(0, planes, 2):
-            pair = block_ref[slot, :, first * nz : (first + 2) * nz, :]
+            pair = rows_ref[:, pl.ds(start + first * nz, 2 * nz), :]
             for step, z, value in planes_of(pair, target * planes + first, 2):
                 out_ref[z, first + step] = value
-        copies[slot][1].wait()
         last = target == groups - 1
-        for _, z, value in planes_of(halo_ref[slot, :, : 2 * nz, :], (target + 1) * planes, 1):
+        for _, z, value in planes_of(rows_ref[:, pl.ds(after, 2 * nz), :], (target + 1) * planes, 1):
             out_ref[z, planes] = jnp.where(last, jnp.zeros_like(value), value)
 
 
@@ -91,22 +78,16 @@
         in_specs=[
             pl.BlockSpec(memory_space=pltpu.SMEM),
             pl.BlockSpec(memory_space=pltpu.VMEM),
-            pl.BlockSpec(memory_space=pl.ANY),
+            pl.BlockSpec(memory_space=pltpu.VMEM),
         ],
         out_specs=[pl.BlockSpec(memory_space=pltpu.VMEM)] * slots,
         out_shape=[jax.ShapeDtypeStruct((nz, planes + 1, count, ny), jnp.bfloat16)] * slots,
-        scratch_shapes=[
-            pltpu.VMEM((slots, count, planes * nz, ny), jnp.bfloat16),
-            pltpu.VMEM((slots, count, HALO_ROWS, ny), jnp.bfloat16),
-            pltpu.SemaphoreType.DMA((slots,)),
-            pltpu.SemaphoreType.DMA((slots,)),
-        ],
         compiler_params=pltpu.CompilerParams(vmem_limit_bytes=VMEM),
         name="fields",
     )(place, positions, rows)
 
 
-def pairs_kernel(groups, count, place_ref, pairs_ref, weights_ref, out_ref, total_ref):
+def pairs_kernel(groups, count, place_ref, pairs_ref, weights_ref, out_ref, both_ref, total_ref):
     total_ref[...] = jnp.zeros_like(total_ref)
     part = count // groups
     ids = []
@@ -129,6 +110,7 @@
             )
 
     out_ref[...] = total_ref[...].astype(jnp.bfloat16)
+    both_ref[...] = (total_ref[...] + jnp.transpose(total_ref[...])).astype(jnp.bfloat16)
 
 
 def pair_matrix(place, pairs, weights, count, groups):
@@ -139,7 +121,7 @@
             pl.BlockSpec(memory_space=pltpu.VMEM),
             pl.BlockSpec(memory_space=pltpu.VMEM),
         ],
-        out_shape=jax.ShapeDtypeStruct((count, count), jnp.bfloat16),
+        out_shape=[jax.ShapeDtypeStruct((count, count), jnp.bfloat16)] * 2,
         scratch_shapes=[pltpu.VMEM((count, count), jnp.float32)],
         compiler_params=pltpu.CompilerParams(vmem_limit_bytes=VMEM),
         cost_estimate=pl.CostEstimate(
@@ -158,34 +140,58 @@
     return jnp.sum(total, axis=0)
 
 
-def inner_kernel(matrix_ref, *refs):
-    blocks, out_ref = refs[:-1], refs[-1]
-    nz, planes, _, ny = blocks[0].shape
-    matrix = matrix_ref[...]
-    count = matrix.shape[0]
+def node_slopes(blocks, x, z):
+    nz = blocks[0].shape[0]
 
     def field(x, z):
         return jnp.concatenate([block[z, x] for block in blocks], axis=0)
+
+    here = field(x, z)
+    ahead = jnp.concatenate([here[:, 1:], jnp.zeros((here.shape[0], 1), here.dtype)], axis=1)
+    slopes = [field(x + 1, z) - here, ahead - here]
+    if z < nz - 1:
+        slopes.append(field(x, z + 1) - here)
+    return slopes
+
+
+def early_kernel(matrix_ref, *refs):
+    blocks, out_ref = refs[:-1], refs[-1]
+    nz, planes, part, _ = blocks[0].shape
+    count = part * len(blocks)
+    matrix = matrix_ref[:count, :count]
 
     @pl.loop(0, planes - 1)
     def _(x):
         for z in range(nz):
-            here = field(x, z)
-            ahead = jnp.concatenate([here[:, 1:], jnp.zeros((count, 1), here.dtype)], axis=1)
-            slopes = [field(x + 1, z) - here, ahead - here]
-            if z < nz - 1:
-                slopes.append(field(x, z + 1) - here)
-            out_ref[x, z] = form(matrix, slopes)
-
-
-def outer_kernel(matrix_ref, inner_ref, conductivity_ref, above_ref, *refs):
+            out_ref[x, z] = form(matrix, node_slopes(blocks, x, z))
+
+
+def late_kernel(early, matrix_ref, both_ref, early_ref, *refs):
     blocks, out_ref = refs[:-1], refs[-1]
-    planes = above_ref.shape[1]
+    nz, planes, part, _ = blocks[0].shape
+    first = early * part
+    matrix = jnp.concatenate([both_ref[first:, :first], matrix_ref[first:, first:]], axis=1)
+
+    @pl.loop(0, planes - 1)
+    def _(x):
+        for z in range(nz):
+            total = None
+            for slope in node_slopes(blocks, x, z):
+                mixed = jnp.dot(matrix, slope, preferred_element_type=jnp.float32)
+                term = slope[first:].astype(jnp.float32) * mixed
+                total = term if total is None else total + term
+            out_ref[x, z] = early_ref[x, z] + jnp.sum(total, axis=0)
+
+
+def outer_kernel(matrix_ref, inner_ref, conductivity_ref, early_ref, late_ref, *refs):
+    blocks, out_ref = refs[:-1], refs[-1]
+    planes = early_ref.shape[1]
     top = blocks[0].shape[0] - 1
     matrix = matrix_ref[...]
     for x in range(planes):
         here = jnp.concatenate([block[top, x] for block in blocks], axis=0)
-        slope = above_ref[:, x].reshape(here.shape) - here
+        above = jnp.concatenate([early_ref[:, x], late_ref[:, x]], axis=0).reshape(here.shape)
+        slope = above - here
         rise = form(matrix, [slope])
         for z in range(top):
             out_ref[x, z] = conductivity_ref[x, z] * inner_ref[x, z]
@@ -197,30 +203,44 @@
     slabs = lax.axis_size("slab")
     count = secondary.shape[0] * groups
     place = jnp.stack([lax.axis_index("elec"), lax.axis_index("slab")])
-    blocks = spread_fields(OFFSETS, place, secondary, positions, groups)
+    blocks = spread_fields(OFFSETS, place, secondary, positions.astype(jnp.float32), groups)
     planes = blocks[0].shape[1] - 1
     blocks = [blocks[0]] + [
         lax.ppermute(block, "elec", [(i, partner(i, offset, groups)) for i in range(groups)])
         for block, offset in zip(blocks[1:], OFFSETS[1:])
     ]
-    matrix = pair_matrix(place, pairs, weights, count, groups)
-    plane = jnp.stack([block[0, :planes] for block in blocks])
-    plane, matrix = lax.optimization_barrier((plane, matrix))
-    above = lax.ppermute(plane, "slab", [(i + 1, i) for i in range(slabs - 1)])
+    matrix, both = pair_matrix(place, pairs, weights, count, groups)
     params = pltpu.CompilerParams(vmem_limit_bytes=VMEM)
+    result = jax.ShapeDtypeStruct(conductivity.shape, jnp.float32)
+
+    def lowest(some):
+        plane = jnp.stack([block[0, :planes] for block in some])
+        return lax.ppermute(plane, "slab", [(i + 1, i) for i in range(slabs - 1)])
+
+    some = lax.optimization_barrier((*blocks[:EARLY], matrix))
+    above = [lowest(some[:-1])]
+    early = pl.pallas_call(
+        early_kernel,
+        out_shape=result,
+        compiler_params=params,
+        cost_estimate=pl.CostEstimate(flops=900000000, bytes_accessed=3000000, transcendentals=0),
+        name="early_slopes",
+    )(matrix, *blocks[:EARLY])
+    rest, early = lax.optimization_barrier((tuple(blocks[EARLY:]), early))
+    above.append(lowest(rest))
     inner = pl.pallas_call(
-        inner_kernel,
-        out_shape=jax.ShapeDtypeStruct(conductivity.shape, jnp.float32),
+        functools.partial(late_kernel, EARLY),
+        out_shape=result,
         compiler_params=params,
-        cost_estimate=pl.CostEstimate(flops=1600000000, bytes_accessed=3000000, transcendentals=0),
-        name="inner_slopes",
-    )(matrix, *blocks)
+        cost_estimate=pl.CostEstimate(flops=700000000, bytes_accessed=3000000, transcendentals=0),
+        name="late_slopes",
+    )(matrix, both, early, *blocks)
     return pl.pallas_call(
         outer_kernel,
-        out_shape=jax.ShapeDtypeStruct(conductivity.shape, jnp.float32),
+        out_shape=result,
         compiler_params=params,
         name="outer_slopes",
-    )(matrix, inner, conductivity, above, *blocks)
+    )(matrix, inner, conductivity, *above, *blocks)
 
 
 def solution(mesh):

time: 53.4 us -> 48.7 us (0.912)
  waiting for transfers between devices: 10.9 us -> 1.68 us
  starting transfers between devices: 18.6 us -> 21.5 us
  Pallas kernels: 21.2 us -> 22.7 us
  other arithmetic: 0.07 us -> 0.77 us
  local copies, waits for them, and re-layouts: 2.38 us -> 1.69 us
    ppermute x7, waiting for transfers between devices: 7.21 us -> 0.15 us  [body(): lax.ppermute(block, 'elec', [(i, partner(i, offset, groups)) for i in ran...]
    ppermute x1 -> x2, starting transfers between devices: 5.18 us -> 8.24 us  [lowest(): return lax.ppermute(plane, 'slab', [(i + 1, i) for i in range(slabs - 1)])]
    ppermute x1 -> x2, waiting for transfers between devices: 3.71 us -> 1.52 us  [lowest(): return lax.ppermute(plane, 'slab', [(i + 1, i) for i in range(slabs - 1)])]
    pallas_call x2 -> x3, Pallas kernels: 5.72 us -> 7.65 us  [the longest x1 3.94 us: body(): pl.pallas_call(early_kernel, out_shape=result, compiler_params=params, co...]
    unnamed x17 -> x13, local copies, waits for them, and re-layouts: 2.37 us -> 1.66 us
    convert_element_type x0 -> x1, other arithmetic: none -> 0.68 us  [body(): positions.astype(jnp.float32)]
    pallas_call x1, Pallas kernels: 3.04 us -> 2.45 us  [spread_fields(): pl.pallas_call(functools.partial(fields_kernel, offsets, groups, nz), in_...]
  transfers between devices with their start and end apart: 8 -> 9, of which waited for: 4 -> 2; matrix products, arithmetic and copies ran while one was open for 0% -> 0% of each run, Pallas kernels for 32% -> 39%
where the time goes in v3:
time: 48.7 us; the launch traced here: 48.5 us
  Pallas kernels  22.7 us (47%)
  starting transfers between devices  21.5 us (44%)
  local copies, waits for them, and re-layouts  1.69 us (3%)
  waiting for transfers between devices  1.68 us (3%)
  other arithmetic  0.77 us (2%)
    ppermute x7, starting transfers between devices, body(): lax.ppermute(block, 'elec', [(i, partner(i, offset, groups)) for i in ran...  13.3 us
    pallas_call x1, Pallas kernels, pair_matrix(): pl.pallas_call(functools.partial(pairs_kernel, groups, count), in_specs=[...  12.6 us
    ppermute x2, starting transfers between devices, lowest(): return lax.ppermute(plane, 'slab', [(i + 1, i) for i in range(slabs - 1)])  8.24 us
    pallas_call x1, Pallas kernels, body(): pl.pallas_call(early_kernel, out_shape=result, compiler_params=params, co...  3.94 us
    pallas_call x1, Pallas kernels, body(): pl.pallas_call(functools.partial(late_kernel, EARLY), out_shape=result, c...  2.63 us
    pallas_call x1, Pallas kernels, spread_fields(): pl.pallas_call(functools.partial(fields_kernel, offsets, groups, nz), in_...  2.45 us
    unnamed x13, local copies, waits for them, and re-layouts  1.66 us
    ppermute x2, waiting for transfers between devices, lowest(): return lax.ppermute(plane, 'slab', [(i + 1, i) for i in range(slabs - 1)])  1.52 us
  transfers between devices with their start and end apart: 9, of which 2 were waited for; matrix products, arithmetic and copies ran while one was open for 0% of the time, Pallas kernels for 39%

profile of v3, /device:TPU:1, one launch (start us, length us, event | category | flops | bytes accessed | tf_op | source)
XLA Modules:
  0.0 48.5 jit_solution(15886383177021455948)
XLA Ops:
  0.0 0.7 %convert_element_type.3.positions_ref = f32[3,32]{1,0:T(4,128)S(1)} convert(s32[3,32]{1,0:T(4,128)} %param.7) | non-fusion elementwise | flops 96 | bytes 768 | tf_op jit(solution)/shard_map/convert_element_type | solution.py:206
  0.7 0.1 pad_add_fusion.place_ref
  0.8 1.6 %copy-done = bf16[32,64,4,128]{3,2,1,0:T(4,128)(2,1)S(1)} copy-done((bf16[32,64,4,128]{3,2,1,0:T(4,128)(2,1)S(1)}, bf16[32,64,4,128]{3,2,1,0:T(4,128)(2,1)}, u32[]{:S(2)}) %copy-start) | copy-done | bytes 2097176
  2.4 2.5 %fields.1 = (bf16[4,9,32,128]{3,2,1,0:T(8,128)(2,1)S(1)}, bf16[4,9,32,128]{3,2,1,0:T(8,128)(2,1)S(1)}, bf16[4,9,32,128]{3,2,1,0:T(8,128)(2,1)S(1)}, bf16[4,9,32,...) custom-call(s32[2]{0:T(128)S(1)} %pad_add_fusion.place_ref, ...), custom_call_target="tpu_custom_call" | custom-call | tf_op jit(solution)/shard_map/fields/pallas_call | solution.py:76
  4.8 3.7 %collective-permute-start.2 = (bf16[4,9,32,128]{3,2,1,0:T(8,128)(2,1)S(1)}, bf16[4,9,32,128]{3,2,1,0:T(8,128)(2,1)S(1)}, u32[]{:S(2)}, u32[]{:S(2)}) collective-permute-start(bf16[4,9,32,128]{3,2,1,0:T(8,128)(2,1)S(1)} %get-tuple-element.29), channel_id=1, source_target_pairs={{0,16},{16,0},{32,48},{48,32},{64,80},{80,64},{96,112},{112,96},{1... | collective-permute-start | bytes 884744 | tf_op jit(solution)/shard_map/ppermute | solution.py:209
  8.5 2.9 %collective-permute-start.3 = (bf16[4,9,32,128]{3,2,1,0:T(8,128)(2,1)S(1)}, bf16[4,9,32,128]{3,2,1,0:T(8,128)(2,1)S(1)}, u32[]{:S(2)}, u32[]{:S(2)}) collective-permute-start(bf16[4,9,32,128]{3,2,1,0:T(8,128)(2,1)S(1)} %get-tuple-element.30), channel_id=1, source_target_pairs={{0,64},{16,80},{32,96},{48,112},{64,0},{80,16},{96,32},{112,48},{1... | collective-permute-start | bytes 884744 | tf_op jit(solution)/shard_map/ppermute | solution.py:209
  11.4 0.0 collective-permute-start.4
  11.4 3.8 %collective-permute-start.5 = (bf16[4,9,32,128]{3,2,1,0:T(8,128)(2,1)S(1)}, bf16[4,9,32,128]{3,2,1,0:T(8,128)(2,1)S(1)}, u32[]{:S(2)}, u32[]{:S(2)}) collective-permute-start(bf16[4,9,32,128]{3,2,1,0:T(8,128)(2,1)S(1)} %get-tuple-element.32), channel_id=1, source_target_pairs={{0,48},{16,32},{32,80},{48,64},{64,112},{80,96},{96,16},{112,0},{1... | collective-permute-start | bytes 884744 | tf_op jit(solution)/shard_map/ppermute | solution.py:209
  15.1 1.4 %collective-permute-start.6 = (bf16[4,9,32,128]{3,2,1,0:T(8,128)(2,1)S(1)}, bf16[4,9,32,128]{3,2,1,0:T(8,128)(2,1)S(1)}, u32[]{:S(2)}, u32[]{:S(2)}) collective-permute-start(bf16[4,9,32,128]{3,2,1,0:T(8,128)(2,1)S(1)} %get-tuple-element.33), channel_id=1, source_target_pairs={{0,96},{16,112},{32,0},{48,16},{64,32},{80,48},{96,64},{112,80},{1... | collective-permute-start | bytes 884744 | tf_op jit(solution)/shard_map/ppermute | solution.py:209
  16.5 12.6 %pair_weights.1 = (bf16[256,256]{1,0:T(8,128)(2,1)S(1)}, bf16[256,256]{1,0:T(8,128)(2,1)S(1)}) custom-call(s32[2]{0:T(128)S(1)} %pad_add_fusion.place_ref, s32[2,32768]{1,0:T(2,128)S(1)} %bitcast.6, f32[1,32768]{1,0:T(1,128)S(1)} %bitcast.7), custom_call_target="tpu_custom_call" | custom-call | flops 8589934592 | bytes 393216 | tf_op jit(solution)/shard_map/pair_weights/pallas_call | solution.py:117
  29.1 0.0 collective-permute-done.2.refs_1_
  29.1 1.5 %collective-permute-start = (bf16[4,9,32,128]{3,2,1,0:T(8,128)(2,1)S(1)}, bf16[4,9,32,128]{3,2,1,0:T(8,128)(2,1)S(1)}, u32[]{:S(2)}, u32[]{:S(2)}) collective-permute-start(bf16[4,9,32,128]{3,2,1,0:T(8,128)(2,1)S(1)} %get-tuple-element.26), channel_id=1, source_target_pairs={{0,112},{16,96},{32,16},{48,0},{64,48},{80,32},{96,80},{112,64},{1... | collective-permute-start | bytes 884744 | tf_op jit(solution)/shard_map/ppermute | solution.py:209
  30.6 0.0 collective-permute-done.3.refs_2_
  30.7 0.1 collective-permute-start.1
  30.7 0.0 collective-permute-done.4.refs_3_
  30.7 0.1 collective-permute-done.6.refs_5_
  31.0 4.2 %collective-permute-start.7 = (bf16[6,8,32,128]{3,2,1,0:T(8,128)(2,1)S(1)}, bf16[6,8,32,128]{3,2,1,0:T(8,128)(2,1)S(1)}, u32[]{:S(2)}, u32[]{:S(2)}) collective-permute-start(bf16[6,8,32,128]{3,2,1,0:T(8,128)(2,1)S(1)} %slice_dynamic-update-slice_fusion), channel_id=1, source_target_pairs={{1,0},{2,1},{3,2},{4,3},{5,4},{6,5},{7,6},{8,7},{9,8},{10,9},{11,1... | collective-permute-start | bytes 1179656 | tf_op jit(solution)/shard_map/ppermute | solution.py:218
  35.2 3.9 %early_slopes.1.early_ref = f32[8,4,128]{2,1,0:T(4,128)S(1)} custom-call(bf16[256,256]{1,0:T(8,128)(2,1)S(1)} %get-tuple-element.24.matrix_ref, bf16[4,9,32,128]{3,2,1,0:T(8,128)(2,1)S(1)} %get-tuple-element.35.refs_0_, bf16[4,9,32,128]{3,2,1,0:T(8,128)(2,1)S(1)} %collective-permute-done.2.refs_1_, ...), custom_call_target="tpu_custom_call" | custom-call | flops 900000000 | bytes 3000000 | tf_op jit(solution)/shard_map/early_slopes/pallas_call | solution.py:222
  39.1 0.0 copy-start.1
  39.2 4.0 %collective-permute-start.8 = (bf16[2,8,32,128]{3,2,1,0:T(8,128)(2,1)S(1)}, bf16[2,8,32,128]{3,2,1,0:T(8,128)(2,1)S(1)}, u32[]{:S(2)}, u32[]{:S(2)}) collective-permute-start(bf16[2,8,32,128]{3,2,1,0:T(8,128)(2,1)S(1)} %pad_maximum_fusion), channel_id=1, source_target_pairs={{1,0},{2,1},{3,2},{4,3},{5,4},{6,5},{7,6},{8,7},{9,8},{10,9},{11,1... | collective-permute-start | bytes 393224 | tf_op jit(solution)/shard_map/ppermute | solution.py:218
  43.2 2.6 %late_slopes.1.inner_ref = f32[8,4,128]{2,1,0:T(4,128)S(1)} custom-call(bf16[256,256]{1,0:T(8,128)(2,1)S(1)} %get-tuple-element.24.matrix_ref, bf16[256,256]{1,0:T(8,128)(2,1)S(1)} %get-tuple-element.25.both_ref, f32[8,4,128]{2,1,0:T(4,128)S(1)} %early_slopes.1.early_ref, bf16[4,9,32,128]{3,2,1,0:T(8,128)(2,1)S(1)} %get-tuple-element.35.refs_0_, ...), custom_call_target="tpu_custom_call" | custom-call | flops 700000000 | bytes 3000000 | tf_op jit(solution)/shard_map/late_slopes/pallas_call | solution.py:231
  45.9 1.5 %collective-permute-done.8.late_ref = bf16[2,8,32,128]{3,2,1,0:T(8,128)(2,1)S(1)} collective-permute-done((bf16[2,8,32,128]{3,2,1,0:T(8,128)(2,1)S(1)}, bf16[2,8,32,128]{3,2,1,0:T(8,128)(2,1)S(1)}, u32[]{:S(2)}, u32[]{:S(2)}) %collective-permute-start.8) | collective-permute-done | bytes 131104 | tf_op jit(solution)/shard_map/ppermute | solution.py:218
  47.4 0.0 collective-permute-done.7.early_ref
  47.4 1.1 %outer_slopes.1 = f32[8,4,128]{2,1,0:T(4,128)} custom-call(bf16[256,256]{1,0:T(8,128)(2,1)S(1)} %get-tuple-element.24.matrix_ref, f32[8,4,128]{2,1,0:T(4,128)S(1)} %late_slopes.1.inner_ref, f32[8,4,128]{2,1,0:T(4,128)S(1)} %copy-done.1, bf16[6,8,32,128]{3,2,1,0:T(8,128)(2,1)S(1)} %collective-permute-done.7.early_ref, ...), custom_call_target="tpu_custom_call" | custom-call | tf_op jit(solution)/shard_map/outer_slopes/pallas_call | solution.py:238
  (18 shorter events, 0.1 us)
Async XLA Ops:
  0.8 1.6 %copy-start = (bf16[32,64,4,128]{3,2,1,0:T(4,128)(2,1)S(1)}, bf16[32,64,4,128]{3,2,1,0:T(4,128)(2,1)}, u32[]{:S(2)}) copy-start(bf16[32,64,4,128]{3,2,1,0:T(4,128)(2,1)} %param.5) | copy-start | bytes 6291460
  2.4 14.2 %copy-start.2 = (s32[32768,2]{0,1:T(2,128)S(1)}, s32[32768,2]{0,1:T(2,128)}, u32[]{:S(2)}) copy-start(s32[32768,2]{0,1:T(2,128)} %param.8) | copy-start | bytes 786436
  2.4 14.2 %copy-start.3 = (f32[32768]{0:T(1024)S(1)}, f32[32768]{0:T(1024)}, u32[]{:S(2)}) copy-start(f32[32768]{0:T(1024)} %param.9) | copy-start | bytes 393220
  4.8 24.3 %collective-permute-start.2 = (bf16[4,9,32,128]{3,2,1,0:T(8,128)(2,1)S(1)}, bf16[4,9,32,128]{3,2,1,0:T(8,128)(2,1)S(1)}, u32[]{:S(2)}, u32[]{:S(2)}) collective-permute-start(bf16[4,9,32,128]{3,2,1,0:T(8,128)(2,1)S(1)} %get-tuple-element.29), channel_id=1, source_target_pairs={{0,16},{16,0},{32,48},{48,32},{64,80},{80,64},{96,112},{112,96},{1... | collective-permute-start | bytes 884744 | tf_op jit(solution)/shard_map/ppermute | solution.py:209
  8.5 22.2 %collective-permute-start.3 = (bf16[4,9,32,128]{3,2,1,0:T(8,128)(2,1)S(1)}, bf16[4,9,32,128]{3,2,1,0:T(8,128)(2,1)S(1)}, u32[]{:S(2)}, u32[]{:S(2)}) collective-permute-start(bf16[4,9,32,128]{3,2,1,0:T(8,128)(2,1)S(1)} %get-tuple-element.30), channel_id=1, source_target_pairs={{0,64},{16,80},{32,96},{48,112},{64,0},{80,16},{96,32},{112,48},{1... | collective-permute-start | bytes 884744 | tf_op jit(solution)/shard_map/ppermute | solution.py:209
  11.4 19.3 %collective-permute-start.4 = (bf16[4,9,32,128]{3,2,1,0:T(8,128)(2,1)S(1)}, bf16[4,9,32,128]{3,2,1,0:T(8,128)(2,1)S(1)}, u32[]{:S(2)}, u32[]{:S(2)}) collective-permute-start(bf16[4,9,32,128]{3,2,1,0:T(8,128)(2,1)S(1)} %get-tuple-element.31), channel_id=1, source_target_pairs={{0,80},{16,64},{32,112},{48,96},{64,16},{80,0},{96,48},{112,32},{1... | collective-permute-start | bytes 884744 | tf_op jit(solution)/shard_map/ppermute | solution.py:209
  11.4 19.3 %collective-permute-start.5 = (bf16[4,9,32,128]{3,2,1,0:T(8,128)(2,1)S(1)}, bf16[4,9,32,128]{3,2,1,0:T(8,128)(2,1)S(1)}, u32[]{:S(2)}, u32[]{:S(2)}) collective-permute-start(bf16[4,9,32,128]{3,2,1,0:T(8,128)(2,1)S(1)} %get-tuple-element.32), channel_id=1, source_target_pairs={{0,48},{16,32},{32,80},{48,64},{64,112},{80,96},{96,16},{112,0},{1... | collective-permute-start | bytes 884744 | tf_op jit(solution)/shard_map/ppermute | solution.py:209
  15.1 15.7 %collective-permute-start.6 = (bf16[4,9,32,128]{3,2,1,0:T(8,128)(2,1)S(1)}, bf16[4,9,32,128]{3,2,1,0:T(8,128)(2,1)S(1)}, u32[]{:S(2)}, u32[]{:S(2)}) collective-permute-start(bf16[4,9,32,128]{3,2,1,0:T(8,128)(2,1)S(1)} %get-tuple-element.33), channel_id=1, source_target_pairs={{0,96},{16,112},{32,0},{48,16},{64,32},{80,48},{96,64},{112,80},{1... | collective-permute-start | bytes 884744 | tf_op jit(solution)/shard_map/ppermute | solution.py:209
  29.1 10.0 %collective-permute-start = (bf16[4,9,32,128]{3,2,1,0:T(8,128)(2,1)S(1)}, bf16[4,9,32,128]{3,2,1,0:T(8,128)(2,1)S(1)}, u32[]{:S(2)}, u32[]{:S(2)}) collective-permute-start(bf16[4,9,32,128]{3,2,1,0:T(8,128)(2,1)S(1)} %get-tuple-element.26), channel_id=1, source_target_pairs={{0,112},{16,96},{32,16},{48,0},{64,48},{80,32},{96,80},{112,64},{1... | collective-permute-start | bytes 884744 | tf_op jit(solution)/shard_map/ppermute | solution.py:209
  30.7 8.5 %collective-permute-start.1 = (bf16[4,9,32,128]{3,2,1,0:T(8,128)(2,1)S(1)}, bf16[4,9,32,128]{3,2,1,0:T(8,128)(2,1)S(1)}, u32[]{:S(2)}, u32[]{:S(2)}) collective-permute-start(bf16[4,9,32,128]{3,2,1,0:T(8,128)(2,1)S(1)} %get-tuple-element.27), channel_id=1, source_target_pairs={{0,32},{16,48},{32,64},{48,80},{64,96},{80,112},{96,0},{112,16},{1... | collective-permute-start | bytes 884744 | tf_op jit(solution)/shard_map/ppermute | solution.py:209
  31.0 16.4 %collective-permute-start.7 = (bf16[6,8,32,128]{3,2,1,0:T(8,128)(2,1)S(1)}, bf16[6,8,32,128]{3,2,1,0:T(8,128)(2,1)S(1)}, u32[]{:S(2)}, u32[]{:S(2)}) collective-permute-start(bf16[6,8,32,128]{3,2,1,0:T(8,128)(2,1)S(1)} %slice_dynamic-update-slice_fusion), channel_id=1, source_target_pairs={{1,0},{2,1},{3,2},{4,3},{5,4},{6,5},{7,6},{8,7},{9,8},{10,9},{11,1... | collective-permute-start | bytes 1179656 | tf_op jit(solution)/shard_map/ppermute | solution.py:218
  39.1 8.3 %copy-start.1 = (f32[8,4,128]{2,1,0:T(4,128)S(1)}, f32[8,4,128]{2,1,0:T(4,128)}, u32[]{:S(2)}) copy-start(f32[8,4,128]{2,1,0:T(4,128)} %conductivity_ref.1) | copy-start | bytes 49156
  39.2 8.2 %collective-permute-start.8 = (bf16[2,8,32,128]{3,2,1,0:T(8,128)(2,1)S(1)}, bf16[2,8,32,128]{3,2,1,0:T(8,128)(2,1)S(1)}, u32[]{:S(2)}, u32[]{:S(2)}) collective-permute-start(bf16[2,8,32,128]{3,2,1,0:T(8,128)(2,1)S(1)} %pad_maximum_fusion), channel_id=1, source_target_pairs={{1,0},{2,1},{3,2},{4,3},{5,4},{6,5},{7,6},{8,7},{9,8},{10,9},{11,1... | collective-permute-start | bytes 393224 | tf_op jit(solution)/shard_map/ppermute | solution.py:218

commit v4 on v3

--- a/solution.py
+++ b/solution.py
@@ -8,7 +8,7 @@
 from jax.sharding import PartitionSpec as P
 
 VMEM = 40 * 1024 * 1024
-PAIR_STEP = 2048
+PAIR_STEP = 4096
 HALO_ROWS = 16
 EARLY = 6
 OFFSETS = [(0, 0), (0, 1), (2, 0), (2, 1), (1, 1), (3, 0), (3, 1), (1, 0)]
@@ -131,13 +131,19 @@
     )(place, pairs.T, weights.reshape(1, -1))
 
 
-def form(matrix, slopes):
-    total = None
-    for slope in slopes:
-        mixed = jnp.dot(matrix, slope, preferred_element_type=jnp.float32)
-        term = slope.astype(jnp.float32) * mixed
-        total = term if total is None else total + term
-    return jnp.sum(total, axis=0)
+def forms(matrix, slopes, first=0):
+    flat = [(key, slope) for key, some in slopes.items() for slope in some]
+    totals = {}
+    for at in range(0, len(flat), 2):
+        pair = flat[at : at + 2]
+        width = pair[0][1].shape[1]
+        mixed = jnp.dot(
+            matrix, jnp.concatenate([slope for _, slope in pair], axis=1), preferred_element_type=jnp.float32
+        )
+        for index, (key, slope) in enumerate(pair):
+            term = slope[first:].astype(jnp.float32) * mixed[:, index * width : (index + 1) * width]
+            totals[key] = totals[key] + term if key in totals else term
+    return {key: jnp.sum(total, axis=0) for key, total in totals.items()}
 
 
 def node_slopes(blocks, x, z):
@@ -160,10 +166,12 @@
     count = part * len(blocks)
     matrix = matrix_ref[:count, :count]
 
-    @pl.loop(0, planes - 1)
-    def _(x):
-        for z in range(nz):
-            out_ref[x, z] = form(matrix, node_slopes(blocks, x, z))
+    @pl.loop(0, (planes - 1) // 2)
+    def _(half):
+        nodes = [(2 * half + step, step, z) for step in range(2) for z in range(nz)]
+        sums = forms(matrix, {(step, z): node_slopes(blocks, x, z) for x, step, z in nodes})
+        for x, step, z in nodes:
+            out_ref[x, z] = sums[step, z]
 
 
 def late_kernel(early, matrix_ref, both_ref, early_ref, *refs):
@@ -172,30 +180,28 @@
     first = early * part
     matrix = jnp.concatenate([both_ref[first:, :first], matrix_ref[first:, first:]], axis=1)
 
-    @pl.loop(0, planes - 1)
-    def _(x):
-        for z in range(nz):
-            total = None
-            for slope in node_slopes(blocks, x, z):
-                mixed = jnp.dot(matrix, slope, preferred_element_type=jnp.float32)
-                term = slope[first:].astype(jnp.float32) * mixed
-                total = term if total is None else total + term
-            out_ref[x, z] = early_ref[x, z] + jnp.sum(total, axis=0)
+    @pl.loop(0, (planes - 1) // 2)
+    def _(half):
+        nodes = [(2 * half + step, step, z) for step in range(2) for z in range(nz)]
+        sums = forms(matrix, {(step, z): node_slopes(blocks, x, z) for x, step, z in nodes}, first)
+        for x, step, z in nodes:
+            out_ref[x, z] = early_ref[x, z] + sums[step, z]
 
 
 def outer_kernel(matrix_ref, inner_ref, conductivity_ref, early_ref, late_ref, *refs):
     blocks, out_ref = refs[:-1], refs[-1]
     planes = early_ref.shape[1]
     top = blocks[0].shape[0] - 1
-    matrix = matrix_ref[...]
+    slopes = {}
     for x in range(planes):
         here = jnp.concatenate([block[top, x] for block in blocks], axis=0)
         above = jnp.concatenate([early_ref[:, x], late_ref[:, x]], axis=0).reshape(here.shape)
-        slope = above - here
-        rise = form(matrix, [slope])
+        slopes[x] = [above - here]
+    rises = forms(matrix_ref[...], slopes)
+    for x in range(planes):
         for z in range(top):
             out_ref[x, z] = conductivity_ref[x, z] * inner_ref[x, z]
-        out_ref[x, top] = conductivity_ref[x, top] * (inner_ref[x, top] + rise)
+        out_ref[x, top] = conductivity_ref[x, top] * (inner_ref[x, top] + rises[x])
 
 
 def body(secondary, conductivity, positions, pairs, weights):
@@ -203,7 +209,9 @@
     slabs = lax.axis_size("slab")
     count = secondary.shape[0] * groups
     place = jnp.stack([lax.axis_index("elec"), lax.axis_index("slab")])
-    blocks = spread_fields(OFFSETS, place, secondary, positions.astype(jnp.float32), groups)
+    nodes = positions.astype(jnp.float32)
+    blocks = list(spread_fields(OFFSETS[1:], place, secondary, nodes, groups))
+    blocks = list(spread_fields(OFFSETS[:1], place, secondary, nodes, groups)) + blocks
     planes = blocks[0].shape[1] - 1
     blocks = [blocks[0]] + [
         lax.ppermute(block, "elec", [(i, partner(i, offset, groups)) for i in range(groups)])

time: 48.7 us -> 47.6 us (0.977)
  Pallas kernels: 22.7 us -> 18.9 us
  waiting for transfers between devices: 1.68 us -> 3.99 us
    pallas_call x1, Pallas kernels: 3.94 us -> 2.18 us  [body(): pl.pallas_call(early_kernel, out_shape=result, compiler_params=params, co...]
    pallas_call x1, Pallas kernels: 12.6 us -> 11 us  [pair_matrix(): pl.pallas_call(functools.partial(pairs_kernel, groups, count), in_specs=[...]
    ppermute x7, waiting for transfers between devices: 0.15 us -> 1.54 us  [body(): lax.ppermute(block, 'elec', [(i, partner(i, offset, groups)) for i in ran...]
    ppermute x2, waiting for transfers between devices: 1.52 us -> 2.44 us  [lowest(): return lax.ppermute(plane, 'slab', [(i + 1, i) for i in range(slabs - 1)])]
    pallas_call x1, Pallas kernels: 2.63 us -> 1.71 us  [body(): pl.pallas_call(functools.partial(late_kernel, EARLY), out_shape=result, c...]
    pallas_call x1 -> x2, Pallas kernels: 2.45 us -> 3.04 us  [spread_fields(): pl.pallas_call(functools.partial(fields_kernel, offsets, groups, nz), in_...]
    unnamed x13 -> x15, local copies, waits for them, and re-layouts: 1.66 us -> 1.67 us
  transfers between devices with their start and end apart: 9 -> 9, of which waited for: 2 -> 4; matrix products, arithmetic and copies ran while one was open for 0% -> 0% of each run, Pallas kernels for 39% -> 33%
where the time goes in v4:
time: 47.6 us; the launch traced here: 47.4 us
  starting transfers between devices  21.9 us (46%)
  Pallas kernels  18.9 us (40%)
  waiting for transfers between devices  3.99 us (8%)
  local copies, waits for them, and re-layouts  1.69 us (4%)
  other arithmetic  0.77 us (2%)
    ppermute x7, starting transfers between devices, body(): lax.ppermute(block, 'elec', [(i, partner(i, offset, groups)) for i in ran...  13.3 us
    pallas_call x1, Pallas kernels, pair_matrix(): pl.pallas_call(functools.partial(pairs_kernel, groups, count), in_specs=[...  11 us
    ppermute x2, starting transfers between devices, lowest(): return lax.ppermute(plane, 'slab', [(i + 1, i) for i in range(slabs - 1)])  8.64 us
    pallas_call x2, Pallas kernels, spread_fields(): pl.pallas_call(functools.partial(fields_kernel, offsets, groups, nz), in_...  3.04 us
    ppermute x2, waiting for transfers between devices, lowest(): return lax.ppermute(plane, 'slab', [(i + 1, i) for i in range(slabs - 1)])  2.44 us
    pallas_call x1, Pallas kernels, body(): pl.pallas_call(early_kernel, out_shape=result, compiler_params=params, co...  2.18 us
    pallas_call x1, Pallas kernels, body(): pl.pallas_call(functools.partial(late_kernel, EARLY), out_shape=result, c...  1.71 us
    unnamed x15, local copies, waits for them, and re-layouts  1.67 us
  transfers between devices with their start and end apart: 9, of which 4 were waited for; matrix products, arithmetic and copies ran while one was open for 0% of the time, Pallas kernels for 33%

profile of v4, /device:TPU:1, one launch (start us, length us, event | category | flops | bytes accessed | tf_op | source)
XLA Modules:
  0.0 47.4 jit_solution(6314591979274345868)
XLA Ops:
  0.0 0.7 %convert_element_type.3.positions_ref = f32[3,32]{1,0:T(4,128)S(1)} convert(s32[3,32]{1,0:T(4,128)} %param.7) | non-fusion elementwise | flops 96 | bytes 768 | tf_op jit(solution)/shard_map/convert_element_type | solution.py:212
  0.7 0.1 pad_add_fusion.place_ref
  0.8 1.6 %copy-done = bf16[32,64,4,128]{3,2,1,0:T(4,128)(2,1)S(1)} copy-done((bf16[32,64,4,128]{3,2,1,0:T(4,128)(2,1)S(1)}, bf16[32,64,4,128]{3,2,1,0:T(4,128)(2,1)}, u32[]{:S(2)}) %copy-start) | copy-done | bytes 2097176
  2.4 2.2 %fields.2 = (bf16[4,9,32,128]{3,2,1,0:T(8,128)(2,1)S(1)}, bf16[4,9,32,128]{3,2,1,0:T(8,128)(2,1)S(1)}, bf16[4,9,32,128]{3,2,1,0:T(8,128)(2,1)S(1)}, bf16[4,9,32,...) custom-call(s32[2]{0:T(128)S(1)} %pad_add_fusion.place_ref, ...), custom_call_target="tpu_custom_call" | custom-call | tf_op jit(solution)/shard_map/fields/pallas_call | solution.py:76
  4.6 3.6 %collective-permute-start.2 = (bf16[4,9,32,128]{3,2,1,0:T(8,128)(2,1)S(1)}, bf16[4,9,32,128]{3,2,1,0:T(8,128)(2,1)S(1)}, u32[]{:S(2)}, u32[]{:S(2)}) collective-permute-start(bf16[4,9,32,128]{3,2,1,0:T(8,128)(2,1)S(1)} %get-tuple-element.27), channel_id=1, source_target_pairs={{0,16},{16,0},{32,48},{48,32},{64,80},{80,64},{96,112},{112,96},{1... | collective-permute-start | bytes 884744 | tf_op jit(solution)/shard_map/ppermute | solution.py:217
  8.2 2.9 %collective-permute-start.3 = (bf16[4,9,32,128]{3,2,1,0:T(8,128)(2,1)S(1)}, bf16[4,9,32,128]{3,2,1,0:T(8,128)(2,1)S(1)}, u32[]{:S(2)}, u32[]{:S(2)}) collective-permute-start(bf16[4,9,32,128]{3,2,1,0:T(8,128)(2,1)S(1)} %get-tuple-element.28), channel_id=1, source_target_pairs={{0,64},{16,80},{32,96},{48,112},{64,0},{80,16},{96,32},{112,48},{1... | collective-permute-start | bytes 884744 | tf_op jit(solution)/shard_map/ppermute | solution.py:217
  11.1 0.0 collective-permute-start.4
  11.1 3.8 %collective-permute-start.5 = (bf16[4,9,32,128]{3,2,1,0:T(8,128)(2,1)S(1)}, bf16[4,9,32,128]{3,2,1,0:T(8,128)(2,1)S(1)}, u32[]{:S(2)}, u32[]{:S(2)}) collective-permute-start(bf16[4,9,32,128]{3,2,1,0:T(8,128)(2,1)S(1)} %get-tuple-element.30), channel_id=1, source_target_pairs={{0,48},{16,32},{32,80},{48,64},{64,112},{80,96},{96,16},{112,0},{1... | collective-permute-start | bytes 884744 | tf_op jit(solution)/shard_map/ppermute | solution.py:217
  14.9 1.4 %collective-permute-start.6 = (bf16[4,9,32,128]{3,2,1,0:T(8,128)(2,1)S(1)}, bf16[4,9,32,128]{3,2,1,0:T(8,128)(2,1)S(1)}, u32[]{:S(2)}, u32[]{:S(2)}) collective-permute-start(bf16[4,9,32,128]{3,2,1,0:T(8,128)(2,1)S(1)} %get-tuple-element.31), channel_id=1, source_target_pairs={{0,96},{16,112},{32,0},{48,16},{64,32},{80,48},{96,64},{112,80},{1... | collective-permute-start | bytes 884744 | tf_op jit(solution)/shard_map/ppermute | solution.py:217
  16.3 11.0 %pair_weights.1 = (bf16[256,256]{1,0:T(8,128)(2,1)S(1)}, bf16[256,256]{1,0:T(8,128)(2,1)S(1)}) custom-call(s32[2]{0:T(128)S(1)} %pad_add_fusion.place_ref, s32[2,32768]{1,0:T(2,128)S(1)} %bitcast.7, f32[1,32768]{1,0:T(1,128)S(1)} %bitcast.8), custom_call_target="tpu_custom_call" | custom-call | flops 8589934592 | bytes 393216 | tf_op jit(solution)/shard_map/pair_weights/pallas_call | solution.py:117
  27.3 0.8 %fields.3.refs_0_ = bf16[4,9,32,128]{3,2,1,0:T(8,128)(2,1)S(1)} custom-call(s32[2]{0:T(128)S(1)} %pad_add_fusion.place_ref, f32[3,32]{1,0:T(4,128)S(1)} %convert_element_type.3.positions_ref, bf16[32,256,128]{2,1,0:T(8,128)(2,1)S(1)} %bitcast.6), custom_call_target="tpu_custom_call" | custom-call | tf_op jit(solution)/shard_map/fields/pallas_call | solution.py:76
  28.1 1.5 %collective-permute-start = (bf16[4,9,32,128]{3,2,1,0:T(8,128)(2,1)S(1)}, bf16[4,9,32,128]{3,2,1,0:T(8,128)(2,1)S(1)}, u32[]{:S(2)}, u32[]{:S(2)}) collective-permute-start(bf16[4,9,32,128]{3,2,1,0:T(8,128)(2,1)S(1)} %get-tuple-element.25), channel_id=1, source_target_pairs={{0,112},{16,96},{32,16},{48,0},{64,48},{80,32},{96,80},{112,64},{1... | collective-permute-start | bytes 884744 | tf_op jit(solution)/shard_map/ppermute | solution.py:217
  29.6 0.0 collective-permute-done.3.refs_2_
  29.6 0.1 collective-permute-start.1
  29.7 0.8 %collective-permute-done.5.refs_4_ = bf16[4,9,32,128]{3,2,1,0:T(8,128)(2,1)S(1)} collective-permute-done((bf16[4,9,32,128]{3,2,1,0:T(8,128)(2,1)S(1)}, bf16[4,9,32,128]{3,2,1,0:T(8,128)(2,1)S(1)}, u32[]{:S(2)}, u32[]{:S(2)}) %collective-permute-start.5) | collective-permute-done | bytes 294944 | tf_op jit(solution)/shard_map/ppermute | solution.py:217
  30.5 0.2 collective-permute-done.6.refs_5_
  30.7 3.5 %collective-permute-start.7 = (bf16[6,8,32,128]{3,2,1,0:T(8,128)(2,1)S(1)}, bf16[6,8,32,128]{3,2,1,0:T(8,128)(2,1)S(1)}, u32[]{:S(2)}, u32[]{:S(2)}) collective-permute-start(bf16[6,8,32,128]{3,2,1,0:T(8,128)(2,1)S(1)} %slice_dynamic-update-slice_fusion), channel_id=1, source_target_pairs={{1,0},{2,1},{3,2},{4,3},{5,4},{6,5},{7,6},{8,7},{9,8},{10,9},{11,1... | collective-permute-start | bytes 1179656 | tf_op jit(solution)/shard_map/ppermute | solution.py:226
  34.2 2.2 %early_slopes.1.early_ref = f32[8,4,128]{2,1,0:T(4,128)S(1)} custom-call(bf16[256,256]{1,0:T(8,128)(2,1)S(1)} %get-tuple-element.23.matrix_ref, bf16[4,9,32,128]{3,2,1,0:T(8,128)(2,1)S(1)} %fields.3.refs_0_, bf16[4,9,32,128]{3,2,1,0:T(8,128)(2,1)S(1)} %collective-permute-done.2.refs_1_, bf16[4,9,32,128]{3,2,1,0:T(8,128)(2,1)S(1)} %collective-permute-done.3.refs_2_, ...), custom_call_target="tpu_custom_call" | custom-call | flops 900000000 | bytes 3000000 | tf_op jit(solution)/shard_map/early_slopes/pallas_call | solution.py:230
  36.4 0.0 copy-start.2
  36.4 0.6 %collective-permute-done.refs_6_ = bf16[4,9,32,128]{3,2,1,0:T(8,128)(2,1)S(1)} collective-permute-done((bf16[4,9,32,128]{3,2,1,0:T(8,128)(2,1)S(1)}, bf16[4,9,32,128]{3,2,1,0:T(8,128)(2,1)S(1)}, u32[]{:S(2)}, u32[]{:S(2)}) %collective-permute-start) | collective-permute-done | bytes 294944 | tf_op jit(solution)/shard_map/ppermute | solution.py:217
  37.0 5.2 %collective-permute-start.8 = (bf16[2,8,32,128]{3,2,1,0:T(8,128)(2,1)S(1)}, bf16[2,8,32,128]{3,2,1,0:T(8,128)(2,1)S(1)}, u32[]{:S(2)}, u32[]{:S(2)}) collective-permute-start(bf16[2,8,32,128]{3,2,1,0:T(8,128)(2,1)S(1)} %pad_maximum_fusion), channel_id=1, source_target_pairs={{1,0},{2,1},{3,2},{4,3},{5,4},{6,5},{7,6},{8,7},{9,8},{10,9},{11,1... | collective-permute-start | bytes 393224 | tf_op jit(solution)/shard_map/ppermute | solution.py:226
  42.2 1.7 %late_slopes.1.inner_ref = f32[8,4,128]{2,1,0:T(4,128)S(1)} custom-call(bf16[256,256]{1,0:T(8,128)(2,1)S(1)} %get-tuple-element.23.matrix_ref, bf16[256,256]{1,0:T(8,128)(2,1)S(1)} %get-tuple-element.24.both_ref, f32[8,4,128]{2,1,0:T(4,128)S(1)} %early_slopes.1.early_ref, bf16[4,9,32,128]{3,2,1,0:T(8,128)(2,1)S(1)} %fields.3.refs_0_, ...), custom_call_target="tpu_custom_call" | custom-call | flops 700000000 | bytes 3000000 | tf_op jit(solution)/shard_map/late_slopes/pallas_call | solution.py:239
  43.9 2.4 %collective-permute-done.8.late_ref = bf16[2,8,32,128]{3,2,1,0:T(8,128)(2,1)S(1)} collective-permute-done((bf16[2,8,32,128]{3,2,1,0:T(8,128)(2,1)S(1)}, bf16[2,8,32,128]{3,2,1,0:T(8,128)(2,1)S(1)}, u32[]{:S(2)}, u32[]{:S(2)}) %collective-permute-start.8) | collective-permute-done | bytes 131104 | tf_op jit(solution)/shard_map/ppermute | solution.py:226
  46.4 1.0 %outer_slopes.1 = f32[8,4,128]{2,1,0:T(4,128)} custom-call(bf16[256,256]{1,0:T(8,128)(2,1)S(1)} %get-tuple-element.23.matrix_ref, f32[8,4,128]{2,1,0:T(4,128)S(1)} %late_slopes.1.inner_ref, f32[8,4,128]{2,1,0:T(4,128)S(1)} %copy-done.2, bf16[6,8,32,128]{3,2,1,0:T(8,128)(2,1)S(1)} %collective-permute-done.7.early_ref, ...), custom_call_target="tpu_custom_call" | custom-call | tf_op jit(solution)/shard_map/outer_slopes/pallas_call | solution.py:246
  (21 shorter events, 0.1 us)
Async XLA Ops:
  0.8 1.6 %copy-start = (bf16[32,64,4,128]{3,2,1,0:T(4,128)(2,1)S(1)}, bf16[32,64,4,128]{3,2,1,0:T(4,128)(2,1)}, u32[]{:S(2)}) copy-start(bf16[32,64,4,128]{3,2,1,0:T(4,128)(2,1)} %param.5) | copy-start | bytes 6291460
  2.4 13.9 %copy-start.3 = (s32[32768,2]{0,1:T(2,128)S(1)}, s32[32768,2]{0,1:T(2,128)}, u32[]{:S(2)}) copy-start(s32[32768,2]{0,1:T(2,128)} %param.8) | copy-start | bytes 786436
  2.4 13.9 %copy-start.4 = (f32[32768]{0:T(1024)S(1)}, f32[32768]{0:T(1024)}, u32[]{:S(2)}) copy-start(f32[32768]{0:T(1024)} %param.9) | copy-start | bytes 393220
  4.6 23.5 %collective-permute-start.2 = (bf16[4,9,32,128]{3,2,1,0:T(8,128)(2,1)S(1)}, bf16[4,9,32,128]{3,2,1,0:T(8,128)(2,1)S(1)}, u32[]{:S(2)}, u32[]{:S(2)}) collective-permute-start(bf16[4,9,32,128]{3,2,1,0:T(8,128)(2,1)S(1)} %get-tuple-element.27), channel_id=1, source_target_pairs={{0,16},{16,0},{32,48},{48,32},{64,80},{80,64},{96,112},{112,96},{1... | collective-permute-start | bytes 884744 | tf_op jit(solution)/shard_map/ppermute | solution.py:217
  8.2 21.4 %collective-permute-start.3 = (bf16[4,9,32,128]{3,2,1,0:T(8,128)(2,1)S(1)}, bf16[4,9,32,128]{3,2,1,0:T(8,128)(2,1)S(1)}, u32[]{:S(2)}, u32[]{:S(2)}) collective-permute-start(bf16[4,9,32,128]{3,2,1,0:T(8,128)(2,1)S(1)} %get-tuple-element.28), channel_id=1, source_target_pairs={{0,64},{16,80},{32,96},{48,112},{64,0},{80,16},{96,32},{112,48},{1... | collective-permute-start | bytes 884744 | tf_op jit(solution)/shard_map/ppermute | solution.py:217
  11.1 18.5 %collective-permute-start.4 = (bf16[4,9,32,128]{3,2,1,0:T(8,128)(2,1)S(1)}, bf16[4,9,32,128]{3,2,1,0:T(8,128)(2,1)S(1)}, u32[]{:S(2)}, u32[]{:S(2)}) collective-permute-start(bf16[4,9,32,128]{3,2,1,0:T(8,128)(2,1)S(1)} %get-tuple-element.29), channel_id=1, source_target_pairs={{0,80},{16,64},{32,112},{48,96},{64,16},{80,0},{96,48},{112,32},{1... | collective-permute-start | bytes 884744 | tf_op jit(solution)/shard_map/ppermute | solution.py:217
  11.1 19.3 %collective-permute-start.5 = (bf16[4,9,32,128]{3,2,1,0:T(8,128)(2,1)S(1)}, bf16[4,9,32,128]{3,2,1,0:T(8,128)(2,1)S(1)}, u32[]{:S(2)}, u32[]{:S(2)}) collective-permute-start(bf16[4,9,32,128]{3,2,1,0:T(8,128)(2,1)S(1)} %get-tuple-element.30), channel_id=1, source_target_pairs={{0,48},{16,32},{32,80},{48,64},{64,112},{80,96},{96,16},{112,0},{1... | collective-permute-start | bytes 884744 | tf_op jit(solution)/shard_map/ppermute | solution.py:217
  14.9 15.7 %collective-permute-start.6 = (bf16[4,9,32,128]{3,2,1,0:T(8,128)(2,1)S(1)}, bf16[4,9,32,128]{3,2,1,0:T(8,128)(2,1)S(1)}, u32[]{:S(2)}, u32[]{:S(2)}) collective-permute-start(bf16[4,9,32,128]{3,2,1,0:T(8,128)(2,1)S(1)} %get-tuple-element.31), channel_id=1, source_target_pairs={{0,96},{16,112},{32,0},{48,16},{64,32},{80,48},{96,64},{112,80},{1... | collective-permute-start | bytes 884744 | tf_op jit(solution)/shard_map/ppermute | solution.py:217
  16.3 11.0 %copy-start.1 = (bf16[32,64,4,128]{3,2,1,0:T(4,128)(2,1)S(1)}, bf16[32,64,4,128]{3,2,1,0:T(4,128)(2,1)}, u32[]{:S(2)}) copy-start(bf16[32,64,4,128]{3,2,1,0:T(4,128)(2,1)} %param.5) | copy-start | bytes 6291460
  28.1 8.9 %collective-permute-start = (bf16[4,9,32,128]{3,2,1,0:T(8,128)(2,1)S(1)}, bf16[4,9,32,128]{3,2,1,0:T(8,128)(2,1)S(1)}, u32[]{:S(2)}, u32[]{:S(2)}) collective-permute-start(bf16[4,9,32,128]{3,2,1,0:T(8,128)(2,1)S(1)} %get-tuple-element.25), channel_id=1, source_target_pairs={{0,112},{16,96},{32,16},{48,0},{64,48},{80,32},{96,80},{112,64},{1... | collective-permute-start | bytes 884744 | tf_op jit(solution)/shard_map/ppermute | solution.py:217
  29.6 7.4 %collective-permute-start.1 = (bf16[4,9,32,128]{3,2,1,0:T(8,128)(2,1)S(1)}, bf16[4,9,32,128]{3,2,1,0:T(8,128)(2,1)S(1)}, u32[]{:S(2)}, u32[]{:S(2)}) collective-permute-start(bf16[4,9,32,128]{3,2,1,0:T(8,128)(2,1)S(1)} %get-tuple-element.26), channel_id=1, source_target_pairs={{0,32},{16,48},{32,64},{48,80},{64,96},{80,112},{96,0},{112,16},{1... | collective-permute-start | bytes 884744 | tf_op jit(solution)/shard_map/ppermute | solution.py:217
  30.7 15.7 %collective-permute-start.7 = (bf16[6,8,32,128]{3,2,1,0:T(8,128)(2,1)S(1)}, bf16[6,8,32,128]{3,2,1,0:T(8,128)(2,1)S(1)}, u32[]{:S(2)}, u32[]{:S(2)}) collective-permute-start(bf16[6,8,32,128]{3,2,1,0:T(8,128)(2,1)S(1)} %slice_dynamic-update-slice_fusion), channel_id=1, source_target_pairs={{1,0},{2,1},{3,2},{4,3},{5,4},{6,5},{7,6},{8,7},{9,8},{10,9},{11,1... | collective-permute-start | bytes 1179656 | tf_op jit(solution)/shard_map/ppermute | solution.py:226
  36.4 10.0 %copy-start.2 = (f32[8,4,128]{2,1,0:T(4,128)S(1)}, f32[8,4,128]{2,1,0:T(4,128)}, u32[]{:S(2)}) copy-start(f32[8,4,128]{2,1,0:T(4,128)} %conductivity_ref.1) | copy-start | bytes 49156
  37.0 9.3 %collective-permute-start.8 = (bf16[2,8,32,128]{3,2,1,0:T(8,128)(2,1)S(1)}, bf16[2,8,32,128]{3,2,1,0:T(8,128)(2,1)S(1)}, u32[]{:S(2)}, u32[]{:S(2)}) collective-permute-start(bf16[2,8,32,128]{3,2,1,0:T(8,128)(2,1)S(1)} %pad_maximum_fusion), channel_id=1, source_target_pairs={{1,0},{2,1},{3,2},{4,3},{5,4},{6,5},{7,6},{8,7},{9,8},{10,9},{11,1... | collective-permute-start | bytes 393224 | tf_op jit(solution)/shard_map/ppermute | solution.py:226

commit v5 on v4

--- a/solution.py
+++ b/solution.py
@@ -174,34 +174,51 @@
             out_ref[x, z] = sums[step, z]
 
 
-def late_kernel(early, matrix_ref, both_ref, early_ref, *refs):
-    blocks, out_ref = refs[:-1], refs[-1]
+def late_kernel(early, matrix_ref, both_ref, early_ref, above_ref, *refs):
+    blocks, (out_ref, mixed_ref) = refs[:-2], refs[-2:]
     nz, planes, part, _ = blocks[0].shape
     first = early * part
     matrix = jnp.concatenate([both_ref[first:, :first], matrix_ref[first:, first:]], axis=1)
+    rows = jnp.concatenate([matrix_ref[:first, :first], both_ref[first:, :first]], axis=0)
+
+    def rise(x):
+        return jnp.concatenate([above_ref[slot, x] - blocks[slot][nz - 1, x] for slot in range(early)], axis=0)
 
     @pl.loop(0, (planes - 1) // 2)
     def _(half):
         nodes = [(2 * half + step, step, z) for step in range(2) for z in range(nz)]
         sums = forms(matrix, {(step, z): node_slopes(blocks, x, z) for x, step, z in nodes}, first)
+        rises = [rise(2 * half + step) for step in range(2)]
+        width = rises[0].shape[1]
+        mixed = jnp.dot(rows, jnp.concatenate(rises, axis=1), preferred_element_type=jnp.float32)
         for x, step, z in nodes:
-            out_ref[x, z] = early_ref[x, z] + sums[step, z]
-
-
-def outer_kernel(matrix_ref, inner_ref, conductivity_ref, early_ref, late_ref, *refs):
+            value = early_ref[x, z] + sums[step, z]
+            if z == nz - 1:
+                own = mixed[:, step * width : (step + 1) * width]
+                value += jnp.sum(rises[step].astype(jnp.float32) * own[:first], axis=0)
+                mixed_ref[x] = own[first:]
+            out_ref[x, z] = value
+
+
+def outer_kernel(early, matrix_ref, inner_ref, mixed_ref, conductivity_ref, above_ref, *refs):
     blocks, out_ref = refs[:-1], refs[-1]
-    planes = early_ref.shape[1]
-    top = blocks[0].shape[0] - 1
-    slopes = {}
-    for x in range(planes):
-        here = jnp.concatenate([block[top, x] for block in blocks], axis=0)
-        above = jnp.concatenate([early_ref[:, x], late_ref[:, x]], axis=0).reshape(here.shape)
-        slopes[x] = [above - here]
-    rises = forms(matrix_ref[...], slopes)
-    for x in range(planes):
-        for z in range(top):
-            out_ref[x, z] = conductivity_ref[x, z] * inner_ref[x, z]
-        out_ref[x, top] = conductivity_ref[x, top] * (inner_ref[x, top] + rises[x])
+    planes = above_ref.shape[1]
+    top, part = blocks[0].shape[0] - 1, blocks[0].shape[2]
+    first = early * part
+    matrix = matrix_ref[first:, first:]
+    for x in range(0, planes, 2):
+        slopes = [
+            jnp.concatenate([above_ref[slot, x + step] - block[top, x + step] for slot, block in enumerate(blocks)], axis=0)
+            for step in range(2)
+        ]
+        width = slopes[0].shape[1]
+        mixed = jnp.dot(matrix, jnp.concatenate(slopes, axis=1), preferred_element_type=jnp.float32)
+        for step in range(2):
+            own = mixed_ref[x + step] + mixed[:, step * width : (step + 1) * width]
+            rise = jnp.sum(slopes[step].astype(jnp.float32) * own, axis=0)
+            for z in range(top):
+                out_ref[x + step, z] = conductivity_ref[x + step, z] * inner_ref[x + step, z]
+            out_ref[x + step, top] = conductivity_ref[x + step, top] * (inner_ref[x + step, top] + rise)
 
 
 def body(secondary, conductivity, positions, pairs, weights):
@@ -226,7 +243,7 @@
         return lax.ppermute(plane, "slab", [(i + 1, i) for i in range(slabs - 1)])
 
     some = lax.optimization_barrier((*blocks[:EARLY], matrix))
-    above = [lowest(some[:-1])]
+    above = lowest(some[:-1])
     early = pl.pallas_call(
         early_kernel,
         out_shape=result,
@@ -235,20 +252,25 @@
         name="early_slopes",
     )(matrix, *blocks[:EARLY])
     rest, early = lax.optimization_barrier((tuple(blocks[EARLY:]), early))
-    above.append(lowest(rest))
-    inner = pl.pallas_call(
+    late_above = lowest(rest)
+    inner, mixed = pl.pallas_call(
         functools.partial(late_kernel, EARLY),
-        out_shape=result,
+        out_shape=[
+            result,
+            jax.ShapeDtypeStruct(
+                (planes, sum(block.shape[2] for block in rest), conductivity.shape[2]), jnp.float32
+            ),
+        ],
         compiler_params=params,
         cost_estimate=pl.CostEstimate(flops=700000000, bytes_accessed=3000000, transcendentals=0),
         name="late_slopes",
-    )(matrix, both, early, *blocks)
+    )(matrix, both, early, above, *blocks)
     return pl.pallas_call(
-        outer_kernel,
+        functools.partial(outer_kernel, EARLY),
         out_shape=result,
         compiler_params=params,
         name="outer_slopes",
-    )(matrix, inner, conductivity, *above, *blocks)
+    )(matrix, inner, mixed, conductivity, late_above, *blocks[EARLY:])
 
 
 def solution(mesh):

time: 47.6 us -> 47.4 us (level)
  transfers between devices with their start and end apart: 9 -> 9, of which waited for: 4 -> 4; matrix products, arithmetic and copies ran while one was open for 0% -> 0% of each run, Pallas kernels for 33% -> 34%
where the time goes in v5:
time: 47.4 us; the launch traced here: 47.2 us
  starting transfers between devices  21.9 us (46%)
  Pallas kernels  19.2 us (41%)
  waiting for transfers between devices  3.54 us (7%)
  local copies, waits for them, and re-layouts  1.69 us (4%)
  other arithmetic  0.77 us (2%)
    ppermute x7, starting transfers between devices, body(): lax.ppermute(block, 'elec', [(i, partner(i, offset, groups)) for i in ran...  13.3 us
    pallas_call x1, Pallas kernels, pair_matrix(): pl.pallas_call(functools.partial(pairs_kernel, groups, count), in_specs=[...  11 us
    ppermute x2, starting transfers between devices, lowest(): return lax.ppermute(plane, 'slab', [(i + 1, i) for i in range(slabs - 1)])  8.64 us
    pallas_call x2, Pallas kernels, spread_fields(): pl.pallas_call(functools.partial(fields_kernel, offsets, groups, nz), in_...  3.04 us
    pallas_call x1, Pallas kernels, body(): pl.pallas_call(early_kernel, out_shape=result, compiler_params=params, co...  2.18 us
    pallas_call x1, Pallas kernels, body(): pl.pallas_call(functools.partial(late_kernel, EARLY), out_shape=[result,...  2.15 us
    ppermute x2, waiting for transfers between devices, lowest(): return lax.ppermute(plane, 'slab', [(i + 1, i) for i in range(slabs - 1)])  1.99 us
    unnamed x15, local copies, waits for them, and re-layouts  1.67 us
  transfers between devices with their start and end apart: 9, of which 4 were waited for; matrix products, arithmetic and copies ran while one was open for 0% of the time, Pallas kernels for 34%

profile of v5, /device:TPU:1, one launch (start us, length us, event | category | flops | bytes accessed | tf_op | source)
XLA Modules:
  0.0 47.2 jit_solution(7351184932774466212)
XLA Ops:
  0.0 0.7 %convert_element_type.3.positions_ref = f32[3,32]{1,0:T(4,128)S(1)} convert(s32[3,32]{1,0:T(4,128)} %param.7) | non-fusion elementwise | flops 96 | bytes 768 | tf_op jit(solution)/shard_map/convert_element_type | solution.py:229
  0.7 0.1 pad_add_fusion.place_ref
  0.8 1.6 %copy-done = bf16[32,64,4,128]{3,2,1,0:T(4,128)(2,1)S(1)} copy-done((bf16[32,64,4,128]{3,2,1,0:T(4,128)(2,1)S(1)}, bf16[32,64,4,128]{3,2,1,0:T(4,128)(2,1)}, u32[]{:S(2)}) %copy-start) | copy-done | bytes 2097176
  2.4 2.2 %fields.2 = (bf16[4,9,32,128]{3,2,1,0:T(8,128)(2,1)S(1)}, bf16[4,9,32,128]{3,2,1,0:T(8,128)(2,1)S(1)}, bf16[4,9,32,128]{3,2,1,0:T(8,128)(2,1)S(1)}, bf16[4,9,32,...) custom-call(s32[2]{0:T(128)S(1)} %pad_add_fusion.place_ref, ...), custom_call_target="tpu_custom_call" | custom-call | tf_op jit(solution)/shard_map/fields/pallas_call | solution.py:76
  4.6 3.6 %collective-permute-start.2 = (bf16[4,9,32,128]{3,2,1,0:T(8,128)(2,1)S(1)}, bf16[4,9,32,128]{3,2,1,0:T(8,128)(2,1)S(1)}, u32[]{:S(2)}, u32[]{:S(2)}) collective-permute-start(bf16[4,9,32,128]{3,2,1,0:T(8,128)(2,1)S(1)} %get-tuple-element.29), channel_id=1, source_target_pairs={{0,16},{16,0},{32,48},{48,32},{64,80},{80,64},{96,112},{112,96},{1... | collective-permute-start | bytes 884744 | tf_op jit(solution)/shard_map/ppermute | solution.py:234
  8.2 2.9 %collective-permute-start.3 = (bf16[4,9,32,128]{3,2,1,0:T(8,128)(2,1)S(1)}, bf16[4,9,32,128]{3,2,1,0:T(8,128)(2,1)S(1)}, u32[]{:S(2)}, u32[]{:S(2)}) collective-permute-start(bf16[4,9,32,128]{3,2,1,0:T(8,128)(2,1)S(1)} %get-tuple-element.30), channel_id=1, source_target_pairs={{0,64},{16,80},{32,96},{48,112},{64,0},{80,16},{96,32},{112,48},{1... | collective-permute-start | bytes 884744 | tf_op jit(solution)/shard_map/ppermute | solution.py:234
  11.1 3.8 %collective-permute-start.5 = (bf16[4,9,32,128]{3,2,1,0:T(8,128)(2,1)S(1)}, bf16[4,9,32,128]{3,2,1,0:T(8,128)(2,1)S(1)}, u32[]{:S(2)}, u32[]{:S(2)}) collective-permute-start(bf16[4,9,32,128]{3,2,1,0:T(8,128)(2,1)S(1)} %get-tuple-element.32), channel_id=1, source_target_pairs={{0,48},{16,32},{32,80},{48,64},{64,112},{80,96},{96,16},{112,0},{1... | collective-permute-start | bytes 884744 | tf_op jit(solution)/shard_map/ppermute | solution.py:234
  14.9 1.4 %collective-permute-start.6 = (bf16[4,9,32,128]{3,2,1,0:T(8,128)(2,1)S(1)}, bf16[4,9,32,128]{3,2,1,0:T(8,128)(2,1)S(1)}, u32[]{:S(2)}, u32[]{:S(2)}) collective-permute-start(bf16[4,9,32,128]{3,2,1,0:T(8,128)(2,1)S(1)} %get-tuple-element.33), channel_id=1, source_target_pairs={{0,96},{16,112},{32,0},{48,16},{64,32},{80,48},{96,64},{112,80},{1... | collective-permute-start | bytes 884744 | tf_op jit(solution)/shard_map/ppermute | solution.py:234
  16.3 11.0 %pair_weights.1 = (bf16[256,256]{1,0:T(8,128)(2,1)S(1)}, bf16[256,256]{1,0:T(8,128)(2,1)S(1)}) custom-call(s32[2]{0:T(128)S(1)} %pad_add_fusion.place_ref, s32[2,32768]{1,0:T(2,128)S(1)} %bitcast.7, f32[1,32768]{1,0:T(1,128)S(1)} %bitcast.8), custom_call_target="tpu_custom_call" | custom-call | flops 8589934592 | bytes 393216 | tf_op jit(solution)/shard_map/pair_weights/pallas_call | solution.py:117
  27.3 0.8 %fields.3.refs_0_ = bf16[4,9,32,128]{3,2,1,0:T(8,128)(2,1)S(1)} custom-call(s32[2]{0:T(128)S(1)} %pad_add_fusion.place_ref, f32[3,32]{1,0:T(4,128)S(1)} %convert_element_type.3.positions_ref, bf16[32,256,128]{2,1,0:T(8,128)(2,1)S(1)} %bitcast.6), custom_call_target="tpu_custom_call" | custom-call | tf_op jit(solution)/shard_map/fields/pallas_call | solution.py:76
  28.1 0.0 collective-permute-done.2.refs_1_
  28.1 1.5 %collective-permute-start = (bf16[4,9,32,128]{3,2,1,0:T(8,128)(2,1)S(1)}, bf16[4,9,32,128]{3,2,1,0:T(8,128)(2,1)S(1)}, u32[]{:S(2)}, u32[]{:S(2)}) collective-permute-start(bf16[4,9,32,128]{3,2,1,0:T(8,128)(2,1)S(1)} %get-tuple-element.27), channel_id=1, source_target_pairs={{0,112},{16,96},{32,16},{48,0},{64,48},{80,32},{96,80},{112,64},{1... | collective-permute-start | bytes 884744 | tf_op jit(solution)/shard_map/ppermute | solution.py:234
  29.6 0.0 collective-permute-done.3.refs_2_
  29.6 0.1 collective-permute-start.1
  29.7 0.8 %collective-permute-done.5.refs_4_ = bf16[4,9,32,128]{3,2,1,0:T(8,128)(2,1)S(1)} collective-permute-done((bf16[4,9,32,128]{3,2,1,0:T(8,128)(2,1)S(1)}, bf16[4,9,32,128]{3,2,1,0:T(8,128)(2,1)S(1)}, u32[]{:S(2)}, u32[]{:S(2)}) %collective-permute-start.5) | collective-permute-done | bytes 294944 | tf_op jit(solution)/shard_map/ppermute | solution.py:234
  30.5 0.2 collective-permute-done.6.refs_5_
  30.7 3.5 %collective-permute-start.7 = (bf16[6,8,32,128]{3,2,1,0:T(8,128)(2,1)S(1)}, bf16[6,8,32,128]{3,2,1,0:T(8,128)(2,1)S(1)}, u32[]{:S(2)}, u32[]{:S(2)}) collective-permute-start(bf16[6,8,32,128]{3,2,1,0:T(8,128)(2,1)S(1)} %slice_dynamic-update-slice_fusion), channel_id=1, source_target_pairs={{1,0},{2,1},{3,2},{4,3},{5,4},{6,5},{7,6},{8,7},{9,8},{10,9},{11,1... | collective-permute-start | bytes 1179656 | tf_op jit(solution)/shard_map/ppermute | solution.py:243
  34.2 2.2 %early_slopes.1.early_ref = f32[8,4,128]{2,1,0:T(4,128)S(1)} custom-call(bf16[256,256]{1,0:T(8,128)(2,1)S(1)} %get-tuple-element.25.matrix_ref, bf16[4,9,32,128]{3,2,1,0:T(8,128)(2,1)S(1)} %fields.3.refs_0_, bf16[4,9,32,128]{3,2,1,0:T(8,128)(2,1)S(1)} %collective-permute-done.2.refs_1_, bf16[4,9,32,128]{3,2,1,0:T(8,128)(2,1)S(1)} %collective-permute-done.3.refs_2_, ...), custom_call_target="tpu_custom_call" | custom-call | flops 900000000 | bytes 3000000 | tf_op jit(solution)/shard_map/early_slopes/pallas_call | solution.py:247
  36.4 0.0 copy-start.2
  36.4 0.6 %collective-permute-done.refs_6_.refs_0_ = bf16[4,9,32,128]{3,2,1,0:T(8,128)(2,1)S(1)} collective-permute-done((bf16[4,9,32,128]{3,2,1,0:T(8,128)(2,1)S(1)}, bf16[4,9,32,128]{3,2,1,0:T(8,128)(2,1)S(1)}, u32[]{:S(2)}, u32[]{:S(2)}) %collective-permute-start) | collective-permute-done | bytes 294944 | tf_op jit(solution)/shard_map/ppermute | solution.py:234
  37.0 5.2 %collective-permute-start.8 = (bf16[2,8,32,128]{3,2,1,0:T(8,128)(2,1)S(1)}, bf16[2,8,32,128]{3,2,1,0:T(8,128)(2,1)S(1)}, u32[]{:S(2)}, u32[]{:S(2)}) collective-permute-start(bf16[2,8,32,128]{3,2,1,0:T(8,128)(2,1)S(1)} %pad_maximum_fusion), channel_id=1, source_target_pairs={{1,0},{2,1},{3,2},{4,3},{5,4},{6,5},{7,6},{8,7},{9,8},{10,9},{11,1... | collective-permute-start | bytes 393224 | tf_op jit(solution)/shard_map/ppermute | solution.py:243
  42.2 2.1 %late_slopes.1 = (f32[8,4,128]{2,1,0:T(4,128)S(1)}, f32[8,64,128]{2,1,0:T(8,128)S(1)}) custom-call(bf16[256,256]{1,0:T(8,128)(2,1)S(1)} %get-tuple-element.25.matrix_ref, bf16[256,256]{1,0:T(8,128)(2,1)S(1)} %get-tuple-element.26.both_ref, f32[8,4,128]{2,1,0:T(4,128)S(1)} %early_slopes.1.early_ref, ...), custom_call_target="tpu_custom_call" | custom-call | flops 700000000 | bytes 3000000 | tf_op jit(solution)/shard_map/late_slopes/pallas_call | solution.py:256
  44.4 2.0 %collective-permute-done.8.above_ref = bf16[2,8,32,128]{3,2,1,0:T(8,128)(2,1)S(1)} collective-permute-done((bf16[2,8,32,128]{3,2,1,0:T(8,128)(2,1)S(1)}, bf16[2,8,32,128]{3,2,1,0:T(8,128)(2,1)S(1)}, u32[]{:S(2)}, u32[]{:S(2)}) %collective-permute-start.8) | collective-permute-done | bytes 131104 | tf_op jit(solution)/shard_map/ppermute | solution.py:243
  46.4 0.8 %outer_slopes.1 = f32[8,4,128]{2,1,0:T(4,128)} custom-call(bf16[256,256]{1,0:T(8,128)(2,1)S(1)} %get-tuple-element.25.matrix_ref, f32[8,4,128]{2,1,0:T(4,128)S(1)} %get-tuple-element.41.inner_ref, f32[8,64,128]{2,1,0:T(8,128)S(1)} %get-tuple-element.42.mixed_ref, f32[8,4,128]{2,1,0:T(4,128)S(1)} %copy-done.2, ...), custom_call_target="tpu_custom_call" | custom-call | tf_op jit(solution)/shard_map/outer_slopes/pallas_call | solution.py:268
  (21 shorter events, 0.1 us)
Async XLA Ops:
  0.8 1.6 %copy-start = (bf16[32,64,4,128]{3,2,1,0:T(4,128)(2,1)S(1)}, bf16[32,64,4,128]{3,2,1,0:T(4,128)(2,1)}, u32[]{:S(2)}) copy-start(bf16[32,64,4,128]{3,2,1,0:T(4,128)(2,1)} %param.5) | copy-start | bytes 6291460
  2.4 13.9 %copy-start.3 = (s32[32768,2]{0,1:T(2,128)S(1)}, s32[32768,2]{0,1:T(2,128)}, u32[]{:S(2)}) copy-start(s32[32768,2]{0,1:T(2,128)} %param.8) | copy-start | bytes 786436
  2.4 13.9 %copy-start.4 = (f32[32768]{0:T(1024)S(1)}, f32[32768]{0:T(1024)}, u32[]{:S(2)}) copy-start(f32[32768]{0:T(1024)} %param.9) | copy-start | bytes 393220
  4.6 23.5 %collective-permute-start.2 = (bf16[4,9,32,128]{3,2,1,0:T(8,128)(2,1)S(1)}, bf16[4,9,32,128]{3,2,1,0:T(8,128)(2,1)S(1)}, u32[]{:S(2)}, u32[]{:S(2)}) collective-permute-start(bf16[4,9,32,128]{3,2,1,0:T(8,128)(2,1)S(1)} %get-tuple-element.29), channel_id=1, source_target_pairs={{0,16},{16,0},{32,48},{48,32},{64,80},{80,64},{96,112},{112,96},{1... | collective-permute-start | bytes 884744 | tf_op jit(solution)/shard_map/ppermute | solution.py:234
  8.2 21.4 %collective-permute-start.3 = (bf16[4,9,32,128]{3,2,1,0:T(8,128)(2,1)S(1)}, bf16[4,9,32,128]{3,2,1,0:T(8,128)(2,1)S(1)}, u32[]{:S(2)}, u32[]{:S(2)}) collective-permute-start(bf16[4,9,32,128]{3,2,1,0:T(8,128)(2,1)S(1)} %get-tuple-element.30), channel_id=1, source_target_pairs={{0,64},{16,80},{32,96},{48,112},{64,0},{80,16},{96,32},{112,48},{1... | collective-permute-start | bytes 884744 | tf_op jit(solution)/shard_map/ppermute | solution.py:234
  11.1 18.5 %collective-permute-start.4 = (bf16[4,9,32,128]{3,2,1,0:T(8,128)(2,1)S(1)}, bf16[4,9,32,128]{3,2,1,0:T(8,128)(2,1)S(1)}, u32[]{:S(2)}, u32[]{:S(2)}) collective-permute-start(bf16[4,9,32,128]{3,2,1,0:T(8,128)(2,1)S(1)} %get-tuple-element.31), channel_id=1, source_target_pairs={{0,80},{16,64},{32,112},{48,96},{64,16},{80,0},{96,48},{112,32},{1... | collective-permute-start | bytes 884744 | tf_op jit(solution)/shard_map/ppermute | solution.py:234
  11.1 19.3 %collective-permute-start.5 = (bf16[4,9,32,128]{3,2,1,0:T(8,128)(2,1)S(1)}, bf16[4,9,32,128]{3,2,1,0:T(8,128)(2,1)S(1)}, u32[]{:S(2)}, u32[]{:S(2)}) collective-permute-start(bf16[4,9,32,128]{3,2,1,0:T(8,128)(2,1)S(1)} %get-tuple-element.32), channel_id=1, source_target_pairs={{0,48},{16,32},{32,80},{48,64},{64,112},{80,96},{96,16},{112,0},{1... | collective-permute-start | bytes 884744 | tf_op jit(solution)/shard_map/ppermute | solution.py:234
  14.9 15.7 %collective-permute-start.6 = (bf16[4,9,32,128]{3,2,1,0:T(8,128)(2,1)S(1)}, bf16[4,9,32,128]{3,2,1,0:T(8,128)(2,1)S(1)}, u32[]{:S(2)}, u32[]{:S(2)}) collective-permute-start(bf16[4,9,32,128]{3,2,1,0:T(8,128)(2,1)S(1)} %get-tuple-element.33), channel_id=1, source_target_pairs={{0,96},{16,112},{32,0},{48,16},{64,32},{80,48},{96,64},{112,80},{1... | collective-permute-start | bytes 884744 | tf_op jit(solution)/shard_map/ppermute | solution.py:234
  16.3 11.0 %copy-start.1 = (bf16[32,64,4,128]{3,2,1,0:T(4,128)(2,1)S(1)}, bf16[32,64,4,128]{3,2,1,0:T(4,128)(2,1)}, u32[]{:S(2)}) copy-start(bf16[32,64,4,128]{3,2,1,0:T(4,128)(2,1)} %param.5) | copy-start | bytes 6291460
  28.1 8.9 %collective-permute-start = (bf16[4,9,32,128]{3,2,1,0:T(8,128)(2,1)S(1)}, bf16[4,9,32,128]{3,2,1,0:T(8,128)(2,1)S(1)}, u32[]{:S(2)}, u32[]{:S(2)}) collective-permute-start(bf16[4,9,32,128]{3,2,1,0:T(8,128)(2,1)S(1)} %get-tuple-element.27), channel_id=1, source_target_pairs={{0,112},{16,96},{32,16},{48,0},{64,48},{80,32},{96,80},{112,64},{1... | collective-permute-start | bytes 884744 | tf_op jit(solution)/shard_map/ppermute | solution.py:234
  29.6 7.4 %collective-permute-start.1 = (bf16[4,9,32,128]{3,2,1,0:T(8,128)(2,1)S(1)}, bf16[4,9,32,128]{3,2,1,0:T(8,128)(2,1)S(1)}, u32[]{:S(2)}, u32[]{:S(2)}) collective-permute-start(bf16[4,9,32,128]{3,2,1,0:T(8,128)(2,1)S(1)} %get-tuple-element.28), channel_id=1, source_target_pairs={{0,32},{16,48},{32,64},{48,80},{64,96},{80,112},{96,0},{112,16},{1... | collective-permute-start | bytes 884744 | tf_op jit(solution)/shard_map/ppermute | solution.py:234
  30.7 11.5 %collective-permute-start.7 = (bf16[6,8,32,128]{3,2,1,0:T(8,128)(2,1)S(1)}, bf16[6,8,32,128]{3,2,1,0:T(8,128)(2,1)S(1)}, u32[]{:S(2)}, u32[]{:S(2)}) collective-permute-start(bf16[6,8,32,128]{3,2,1,0:T(8,128)(2,1)S(1)} %slice_dynamic-update-slice_fusion), channel_id=1, source_target_pairs={{1,0},{2,1},{3,2},{4,3},{5,4},{6,5},{7,6},{8,7},{9,8},{10,9},{11,1... | collective-permute-start | bytes 1179656 | tf_op jit(solution)/shard_map/ppermute | solution.py:243
  36.4 10.0 %copy-start.2 = (f32[8,4,128]{2,1,0:T(4,128)S(1)}, f32[8,4,128]{2,1,0:T(4,128)}, u32[]{:S(2)}) copy-start(f32[8,4,128]{2,1,0:T(4,128)} %conductivity_ref.1) | copy-start | bytes 49156
  37.0 9.3 %collective-permute-start.8 = (bf16[2,8,32,128]{3,2,1,0:T(8,128)(2,1)S(1)}, bf16[2,8,32,128]{3,2,1,0:T(8,128)(2,1)S(1)}, u32[]{:S(2)}, u32[]{:S(2)}) collective-permute-start(bf16[2,8,32,128]{3,2,1,0:T(8,128)(2,1)S(1)} %pad_maximum_fusion), channel_id=1, source_target_pairs={{1,0},{2,1},{3,2},{4,3},{5,4},{6,5},{7,6},{8,7},{9,8},{10,9},{11,1... | collective-permute-start | bytes 393224 | tf_op jit(solution)/shard_map/ppermute | solution.py:243

commit v6 on v5

--- a/solution.py
+++ b/solution.py
@@ -8,10 +8,10 @@
 from jax.sharding import PartitionSpec as P
 
 VMEM = 40 * 1024 * 1024
-PAIR_STEP = 4096
+PAIR_STEP = 8192
 HALO_ROWS = 16
 EARLY = 6
-OFFSETS = [(0, 0), (0, 1), (2, 0), (2, 1), (1, 1), (3, 0), (3, 1), (1, 0)]
+OFFSETS = [(0, 0), (2, 0), (0, 1), (2, 1), (1, 1), (3, 0), (3, 1), (1, 0)]
 
 
 def partner(me, offset, groups):

time: 47.4 us -> 46.9 us (0.989)
  Pallas kernels: 19.2 us -> 18.4 us
    pallas_call x1, Pallas kernels: 11 us -> 10.2 us  [pair_matrix(): pl.pallas_call(functools.partial(pairs_kernel, groups, count), in_specs=[...]
  transfers between devices with their start and end apart: 9 -> 9, of which waited for: 4 -> 3; matrix products, arithmetic and copies ran while one was open for 0% -> 0% of each run, Pallas kernels for 34% -> 33%
where the time goes in v6:
time: 46.9 us; the launch traced here: 46.4 us
  starting transfers between devices  21.7 us (46%)
  Pallas kernels  18.4 us (39%)
  waiting for transfers between devices  3.72 us (8%)
  local copies, waits for them, and re-layouts  1.7 us (4%)
  other arithmetic  0.77 us (2%)
    ppermute x7, starting transfers between devices, body(): lax.ppermute(block, 'elec', [(i, partner(i, offset, groups)) for i in ran...  13.3 us
    pallas_call x1, Pallas kernels, pair_matrix(): pl.pallas_call(functools.partial(pairs_kernel, groups, count), in_specs=[...  10.2 us
    ppermute x2, starting transfers between devices, lowest(): return lax.ppermute(plane, 'slab', [(i + 1, i) for i in range(slabs - 1)])  8.42 us
    pallas_call x2, Pallas kernels, spread_fields(): pl.pallas_call(functools.partial(fields_kernel, offsets, groups, nz), in_...  3.03 us
    pallas_call x1, Pallas kernels, body(): pl.pallas_call(early_kernel, out_shape=result, compiler_params=params, co...  2.18 us
    pallas_call x1, Pallas kernels, body(): pl.pallas_call(functools.partial(late_kernel, EARLY), out_shape=[result,...  2.14 us
    ppermute x2, waiting for transfers between devices, lowest(): return lax.ppermute(plane, 'slab', [(i + 1, i) for i in range(slabs - 1)])  2.01 us
    ppermute x7, waiting for transfers between devices, body(): lax.ppermute(block, 'elec', [(i, partner(i, offset, groups)) for i in ran...  1.72 us
  transfers between devices with their start and end apart: 9, of which 3 were waited for; matrix products, arithmetic and copies ran while one was open for 0% of the time, Pallas kernels for 33%

profile of v6, /device:TPU:1, one launch (start us, length us, event | category | flops | bytes accessed | tf_op | source)
XLA Modules:
  0.0 46.4 jit_solution(16846751884258653521)
XLA Ops:
  0.0 0.7 %convert_element_type.3.positions_ref = f32[3,32]{1,0:T(4,128)S(1)} convert(s32[3,32]{1,0:T(4,128)} %param.7) | non-fusion elementwise | flops 96 | bytes 768 | tf_op jit(solution)/shard_map/convert_element_type | solution.py:229
  0.7 0.1 pad_add_fusion.place_ref
  0.8 1.6 %copy-done = bf16[32,64,4,128]{3,2,1,0:T(4,128)(2,1)S(1)} copy-done((bf16[32,64,4,128]{3,2,1,0:T(4,128)(2,1)S(1)}, bf16[32,64,4,128]{3,2,1,0:T(4,128)(2,1)}, u32[]{:S(2)}) %copy-start) | copy-done | bytes 2097176
  2.4 2.2 %fields.2 = (bf16[4,9,32,128]{3,2,1,0:T(8,128)(2,1)S(1)}, bf16[4,9,32,128]{3,2,1,0:T(8,128)(2,1)S(1)}, bf16[4,9,32,128]{3,2,1,0:T(8,128)(2,1)S(1)}, bf16[4,9,32,...) custom-call(s32[2]{0:T(128)S(1)} %pad_add_fusion.place_ref, ...), custom_call_target="tpu_custom_call" | custom-call | tf_op jit(solution)/shard_map/fields/pallas_call | solution.py:76
  4.6 3.8 %collective-permute-start.2 = (bf16[4,9,32,128]{3,2,1,0:T(8,128)(2,1)S(1)}, bf16[4,9,32,128]{3,2,1,0:T(8,128)(2,1)S(1)}, u32[]{:S(2)}, u32[]{:S(2)}) collective-permute-start(bf16[4,9,32,128]{3,2,1,0:T(8,128)(2,1)S(1)} %get-tuple-element.29), channel_id=1, source_target_pairs={{0,64},{16,80},{32,96},{48,112},{64,0},{80,16},{96,32},{112,48},{1... | collective-permute-start | bytes 884744 | tf_op jit(solution)/shard_map/ppermute | solution.py:234
  8.4 2.7 %collective-permute-start.3 = (bf16[4,9,32,128]{3,2,1,0:T(8,128)(2,1)S(1)}, bf16[4,9,32,128]{3,2,1,0:T(8,128)(2,1)S(1)}, u32[]{:S(2)}, u32[]{:S(2)}) collective-permute-start(bf16[4,9,32,128]{3,2,1,0:T(8,128)(2,1)S(1)} %get-tuple-element.30), channel_id=1, source_target_pairs={{0,16},{16,0},{32,48},{48,32},{64,80},{80,64},{96,112},{112,96},{1... | collective-permute-start | bytes 884744 | tf_op jit(solution)/shard_map/ppermute | solution.py:234
  11.1 0.0 collective-permute-start.4
  11.2 3.7 %collective-permute-start.5 = (bf16[4,9,32,128]{3,2,1,0:T(8,128)(2,1)S(1)}, bf16[4,9,32,128]{3,2,1,0:T(8,128)(2,1)S(1)}, u32[]{:S(2)}, u32[]{:S(2)}) collective-permute-start(bf16[4,9,32,128]{3,2,1,0:T(8,128)(2,1)S(1)} %get-tuple-element.32), channel_id=1, source_target_pairs={{0,48},{16,32},{32,80},{48,64},{64,112},{80,96},{96,16},{112,0},{1... | collective-permute-start | bytes 884744 | tf_op jit(solution)/shard_map/ppermute | solution.py:234
  14.9 1.4 %collective-permute-start.6 = (bf16[4,9,32,128]{3,2,1,0:T(8,128)(2,1)S(1)}, bf16[4,9,32,128]{3,2,1,0:T(8,128)(2,1)S(1)}, u32[]{:S(2)}, u32[]{:S(2)}) collective-permute-start(bf16[4,9,32,128]{3,2,1,0:T(8,128)(2,1)S(1)} %get-tuple-element.33), channel_id=1, source_target_pairs={{0,96},{16,112},{32,0},{48,16},{64,32},{80,48},{96,64},{112,80},{1... | collective-permute-start | bytes 884744 | tf_op jit(solution)/shard_map/ppermute | solution.py:234
  16.3 10.2 %pair_weights.1 = (bf16[256,256]{1,0:T(8,128)(2,1)S(1)}, bf16[256,256]{1,0:T(8,128)(2,1)S(1)}) custom-call(s32[2]{0:T(128)S(1)} %pad_add_fusion.place_ref, s32[2,32768]{1,0:T(2,128)S(1)} %bitcast.7, f32[1,32768]{1,0:T(1,128)S(1)} %bitcast.8), custom_call_target="tpu_custom_call" | custom-call | flops 8589934592 | bytes 393216 | tf_op jit(solution)/shard_map/pair_weights/pallas_call | solution.py:117
  26.5 0.8 %fields.3.refs_0_ = bf16[4,9,32,128]{3,2,1,0:T(8,128)(2,1)S(1)} custom-call(s32[2]{0:T(128)S(1)} %pad_add_fusion.place_ref, f32[3,32]{1,0:T(4,128)S(1)} %convert_element_type.3.positions_ref, bf16[32,256,128]{2,1,0:T(8,128)(2,1)S(1)} %bitcast.6), custom_call_target="tpu_custom_call" | custom-call | tf_op jit(solution)/shard_map/fields/pallas_call | solution.py:76
  27.3 1.5 %collective-permute-start = (bf16[4,9,32,128]{3,2,1,0:T(8,128)(2,1)S(1)}, bf16[4,9,32,128]{3,2,1,0:T(8,128)(2,1)S(1)}, u32[]{:S(2)}, u32[]{:S(2)}) collective-permute-start(bf16[4,9,32,128]{3,2,1,0:T(8,128)(2,1)S(1)} %get-tuple-element.27), channel_id=1, source_target_pairs={{0,112},{16,96},{32,16},{48,0},{64,48},{80,32},{96,80},{112,64},{1... | collective-permute-start | bytes 884744 | tf_op jit(solution)/shard_map/ppermute | solution.py:234
  28.8 0.0 collective-permute-done.3.refs_2_
  28.8 0.1 collective-permute-start.1
  28.9 1.7 %collective-permute-done.5.refs_4_ = bf16[4,9,32,128]{3,2,1,0:T(8,128)(2,1)S(1)} collective-permute-done((bf16[4,9,32,128]{3,2,1,0:T(8,128)(2,1)S(1)}, bf16[4,9,32,128]{3,2,1,0:T(8,128)(2,1)S(1)}, u32[]{:S(2)}, u32[]{:S(2)}) %collective-permute-start.5) | collective-permute-done | bytes 294944 | tf_op jit(solution)/shard_map/ppermute | solution.py:234
  30.6 0.0 collective-permute-done.6.refs_5_
  30.7 3.8 %collective-permute-start.7 = (bf16[6,8,32,128]{3,2,1,0:T(8,128)(2,1)S(1)}, bf16[6,8,32,128]{3,2,1,0:T(8,128)(2,1)S(1)}, u32[]{:S(2)}, u32[]{:S(2)}) collective-permute-start(bf16[6,8,32,128]{3,2,1,0:T(8,128)(2,1)S(1)} %slice_dynamic-update-slice_fusion), channel_id=1, source_target_pairs={{1,0},{2,1},{3,2},{4,3},{5,4},{6,5},{7,6},{8,7},{9,8},{10,9},{11,1... | collective-permute-start | bytes 1179656 | tf_op jit(solution)/shard_map/ppermute | solution.py:243
  34.5 2.2 %early_slopes.1.early_ref = f32[8,4,128]{2,1,0:T(4,128)S(1)} custom-call(bf16[256,256]{1,0:T(8,128)(2,1)S(1)} %get-tuple-element.25.matrix_ref, bf16[4,9,32,128]{3,2,1,0:T(8,128)(2,1)S(1)} %fields.3.refs_0_, bf16[4,9,32,128]{3,2,1,0:T(8,128)(2,1)S(1)} %collective-permute-done.2.refs_1_, bf16[4,9,32,128]{3,2,1,0:T(8,128)(2,1)S(1)} %collective-permute-done.3.refs_2_, ...), custom_call_target="tpu_custom_call" | custom-call | flops 900000000 | bytes 3000000 | tf_op jit(solution)/shard_map/early_slopes/pallas_call | solution.py:247
  36.7 0.0 copy-start.2
  36.8 4.6 %collective-permute-start.8 = (bf16[2,8,32,128]{3,2,1,0:T(8,128)(2,1)S(1)}, bf16[2,8,32,128]{3,2,1,0:T(8,128)(2,1)S(1)}, u32[]{:S(2)}, u32[]{:S(2)}) collective-permute-start(bf16[2,8,32,128]{3,2,1,0:T(8,128)(2,1)S(1)} %pad_maximum_fusion), channel_id=1, source_target_pairs={{1,0},{2,1},{3,2},{4,3},{5,4},{6,5},{7,6},{8,7},{9,8},{10,9},{11,1... | collective-permute-start | bytes 393224 | tf_op jit(solution)/shard_map/ppermute | solution.py:243
  41.4 0.1 collective-permute-done.7.above_ref
  41.5 2.1 %late_slopes.1 = (f32[8,4,128]{2,1,0:T(4,128)S(1)}, f32[8,64,128]{2,1,0:T(8,128)S(1)}) custom-call(bf16[256,256]{1,0:T(8,128)(2,1)S(1)} %get-tuple-element.25.matrix_ref, bf16[256,256]{1,0:T(8,128)(2,1)S(1)} %get-tuple-element.26.both_ref, f32[8,4,128]{2,1,0:T(4,128)S(1)} %early_slopes.1.early_ref, ...), custom_call_target="tpu_custom_call" | custom-call | flops 700000000 | bytes 3000000 | tf_op jit(solution)/shard_map/late_slopes/pallas_call | solution.py:256
  43.6 1.9 %collective-permute-done.8.above_ref = bf16[2,8,32,128]{3,2,1,0:T(8,128)(2,1)S(1)} collective-permute-done((bf16[2,8,32,128]{3,2,1,0:T(8,128)(2,1)S(1)}, bf16[2,8,32,128]{3,2,1,0:T(8,128)(2,1)S(1)}, u32[]{:S(2)}, u32[]{:S(2)}) %collective-permute-start.8) | collective-permute-done | bytes 131104 | tf_op jit(solution)/shard_map/ppermute | solution.py:243
  45.6 0.8 %outer_slopes.1 = f32[8,4,128]{2,1,0:T(4,128)} custom-call(bf16[256,256]{1,0:T(8,128)(2,1)S(1)} %get-tuple-element.25.matrix_ref, f32[8,4,128]{2,1,0:T(4,128)S(1)} %get-tuple-element.41.inner_ref, f32[8,64,128]{2,1,0:T(8,128)S(1)} %get-tuple-element.42.mixed_ref, f32[8,4,128]{2,1,0:T(4,128)S(1)} %copy-done.2, ...), custom_call_target="tpu_custom_call" | custom-call | tf_op jit(solution)/shard_map/outer_slopes/pallas_call | solution.py:268
  (21 shorter events, 0.1 us)
Async XLA Ops:
  0.8 1.6 %copy-start = (bf16[32,64,4,128]{3,2,1,0:T(4,128)(2,1)S(1)}, bf16[32,64,4,128]{3,2,1,0:T(4,128)(2,1)}, u32[]{:S(2)}) copy-start(bf16[32,64,4,128]{3,2,1,0:T(4,128)(2,1)} %param.5) | copy-start | bytes 6291460
  2.4 14.0 %copy-start.3 = (s32[32768,2]{0,1:T(2,128)S(1)}, s32[32768,2]{0,1:T(2,128)}, u32[]{:S(2)}) copy-start(s32[32768,2]{0,1:T(2,128)} %param.8) | copy-start | bytes 786436
  2.4 14.0 %copy-start.4 = (f32[32768]{0:T(1024)S(1)}, f32[32768]{0:T(1024)}, u32[]{:S(2)}) copy-start(f32[32768]{0:T(1024)} %param.9) | copy-start | bytes 393220
  4.6 22.7 %collective-permute-start.2 = (bf16[4,9,32,128]{3,2,1,0:T(8,128)(2,1)S(1)}, bf16[4,9,32,128]{3,2,1,0:T(8,128)(2,1)S(1)}, u32[]{:S(2)}, u32[]{:S(2)}) collective-permute-start(bf16[4,9,32,128]{3,2,1,0:T(8,128)(2,1)S(1)} %get-tuple-element.29), channel_id=1, source_target_pairs={{0,64},{16,80},{32,96},{48,112},{64,0},{80,16},{96,32},{112,48},{1... | collective-permute-start | bytes 884744 | tf_op jit(solution)/shard_map/ppermute | solution.py:234
  8.4 20.4 %collective-permute-start.3 = (bf16[4,9,32,128]{3,2,1,0:T(8,128)(2,1)S(1)}, bf16[4,9,32,128]{3,2,1,0:T(8,128)(2,1)S(1)}, u32[]{:S(2)}, u32[]{:S(2)}) collective-permute-start(bf16[4,9,32,128]{3,2,1,0:T(8,128)(2,1)S(1)} %get-tuple-element.30), channel_id=1, source_target_pairs={{0,16},{16,0},{32,48},{48,32},{64,80},{80,64},{96,112},{112,96},{1... | collective-permute-start | bytes 884744 | tf_op jit(solution)/shard_map/ppermute | solution.py:234
  11.1 17.7 %collective-permute-start.4 = (bf16[4,9,32,128]{3,2,1,0:T(8,128)(2,1)S(1)}, bf16[4,9,32,128]{3,2,1,0:T(8,128)(2,1)S(1)}, u32[]{:S(2)}, u32[]{:S(2)}) collective-permute-start(bf16[4,9,32,128]{3,2,1,0:T(8,128)(2,1)S(1)} %get-tuple-element.31), channel_id=1, source_target_pairs={{0,80},{16,64},{32,112},{48,96},{64,16},{80,0},{96,48},{112,32},{1... | collective-permute-start | bytes 884744 | tf_op jit(solution)/shard_map/ppermute | solution.py:234
  11.2 19.4 %collective-permute-start.5 = (bf16[4,9,32,128]{3,2,1,0:T(8,128)(2,1)S(1)}, bf16[4,9,32,128]{3,2,1,0:T(8,128)(2,1)S(1)}, u32[]{:S(2)}, u32[]{:S(2)}) collective-permute-start(bf16[4,9,32,128]{3,2,1,0:T(8,128)(2,1)S(1)} %get-tuple-element.32), channel_id=1, source_target_pairs={{0,48},{16,32},{32,80},{48,64},{64,112},{80,96},{96,16},{112,0},{1... | collective-permute-start | bytes 884744 | tf_op jit(solution)/shard_map/ppermute | solution.py:234
  14.9 15.7 %collective-permute-start.6 = (bf16[4,9,32,128]{3,2,1,0:T(8,128)(2,1)S(1)}, bf16[4,9,32,128]{3,2,1,0:T(8,128)(2,1)S(1)}, u32[]{:S(2)}, u32[]{:S(2)}) collective-permute-start(bf16[4,9,32,128]{3,2,1,0:T(8,128)(2,1)S(1)} %get-tuple-element.33), channel_id=1, source_target_pairs={{0,96},{16,112},{32,0},{48,16},{64,32},{80,48},{96,64},{112,80},{1... | collective-permute-start | bytes 884744 | tf_op jit(solution)/shard_map/ppermute | solution.py:234
  16.3 10.2 %copy-start.1 = (bf16[32,64,4,128]{3,2,1,0:T(4,128)(2,1)S(1)}, bf16[32,64,4,128]{3,2,1,0:T(4,128)(2,1)}, u32[]{:S(2)}) copy-start(bf16[32,64,4,128]{3,2,1,0:T(4,128)(2,1)} %param.5) | copy-start | bytes 6291460
  27.3 9.4 %collective-permute-start = (bf16[4,9,32,128]{3,2,1,0:T(8,128)(2,1)S(1)}, bf16[4,9,32,128]{3,2,1,0:T(8,128)(2,1)S(1)}, u32[]{:S(2)}, u32[]{:S(2)}) collective-permute-start(bf16[4,9,32,128]{3,2,1,0:T(8,128)(2,1)S(1)} %get-tuple-element.27), channel_id=1, source_target_pairs={{0,112},{16,96},{32,16},{48,0},{64,48},{80,32},{96,80},{112,64},{1... | collective-permute-start | bytes 884744 | tf_op jit(solution)/shard_map/ppermute | solution.py:234
  28.8 7.9 %collective-permute-start.1 = (bf16[4,9,32,128]{3,2,1,0:T(8,128)(2,1)S(1)}, bf16[4,9,32,128]{3,2,1,0:T(8,128)(2,1)S(1)}, u32[]{:S(2)}, u32[]{:S(2)}) collective-permute-start(bf16[4,9,32,128]{3,2,1,0:T(8,128)(2,1)S(1)} %get-tuple-element.28), channel_id=1, source_target_pairs={{0,32},{16,48},{32,64},{48,80},{64,96},{80,112},{96,0},{112,16},{1... | collective-permute-start | bytes 884744 | tf_op jit(solution)/shard_map/ppermute | solution.py:234
  30.7 10.8 %collective-permute-start.7 = (bf16[6,8,32,128]{3,2,1,0:T(8,128)(2,1)S(1)}, bf16[6,8,32,128]{3,2,1,0:T(8,128)(2,1)S(1)}, u32[]{:S(2)}, u32[]{:S(2)}) collective-permute-start(bf16[6,8,32,128]{3,2,1,0:T(8,128)(2,1)S(1)} %slice_dynamic-update-slice_fusion), channel_id=1, source_target_pairs={{1,0},{2,1},{3,2},{4,3},{5,4},{6,5},{7,6},{8,7},{9,8},{10,9},{11,1... | collective-permute-start | bytes 1179656 | tf_op jit(solution)/shard_map/ppermute | solution.py:243
  36.7 8.9 %copy-start.2 = (f32[8,4,128]{2,1,0:T(4,128)S(1)}, f32[8,4,128]{2,1,0:T(4,128)}, u32[]{:S(2)}) copy-start(f32[8,4,128]{2,1,0:T(4,128)} %conductivity_ref.1) | copy-start | bytes 49156
  36.8 8.8 %collective-permute-start.8 = (bf16[2,8,32,128]{3,2,1,0:T(8,128)(2,1)S(1)}, bf16[2,8,32,128]{3,2,1,0:T(8,128)(2,1)S(1)}, u32[]{:S(2)}, u32[]{:S(2)}) collective-permute-start(bf16[2,8,32,128]{3,2,1,0:T(8,128)(2,1)S(1)} %pad_maximum_fusion), channel_id=1, source_target_pairs={{1,0},{2,1},{3,2},{4,3},{5,4},{6,5},{7,6},{8,7},{9,8},{10,9},{11,1... | collective-permute-start | bytes 393224 | tf_op jit(solution)/shard_map/ppermute | solution.py:243

commit v7 on v6

--- a/solution.py
+++ b/solution.py
@@ -11,7 +11,7 @@
 PAIR_STEP = 8192
 HALO_ROWS = 16
 EARLY = 6
-OFFSETS = [(0, 0), (2, 0), (0, 1), (2, 1), (1, 1), (3, 0), (3, 1), (1, 0)]
+OFFSETS = [(0, 0), (1, 1), (3, 0), (0, 1), (2, 0), (2, 1), (3, 1), (1, 0)]
 
 
 def partner(me, offset, groups):

time: 46.9 us -> 46.7 us (level)
  transfers between devices with their start and end apart: 9 -> 9, of which waited for: 3 -> 2; matrix products, arithmetic and copies ran while one was open for 0% -> 0% of each run, Pallas kernels for 33% -> 33%
where the time goes in v7:
time: 46.7 us; the launch traced here: 46.5 us
  starting transfers between devices  21.5 us (46%)
  Pallas kernels  18.4 us (39%)
  waiting for transfers between devices  3.97 us (9%)
  local copies, waits for them, and re-layouts  1.7 us (4%)
  other arithmetic  0.77 us (2%)
    ppermute x7, starting transfers between devices, body(): lax.ppermute(block, 'elec', [(i, partner(i, offset, groups)) for i in ran...  13.4 us
    pallas_call x1, Pallas kernels, pair_matrix(): pl.pallas_call(functools.partial(pairs_kernel, groups, count), in_specs=[...  10.2 us
    ppermute x2, starting transfers between devices, lowest(): return lax.ppermute(plane, 'slab', [(i + 1, i) for i in range(slabs - 1)])  8.17 us
    pallas_call x2, Pallas kernels, spread_fields(): pl.pallas_call(functools.partial(fields_kernel, offsets, groups, nz), in_...  3.04 us
    pallas_call x1, Pallas kernels, body(): pl.pallas_call(early_kernel, out_shape=result, compiler_params=params, co...  2.18 us
    pallas_call x1, Pallas kernels, body(): pl.pallas_call(functools.partial(late_kernel, EARLY), out_shape=[result,...  2.14 us
    ppermute x2, waiting for transfers between devices, lowest(): return lax.ppermute(plane, 'slab', [(i + 1, i) for i in range(slabs - 1)])  2.08 us
    ppermute x7, waiting for transfers between devices, body(): lax.ppermute(block, 'elec', [(i, partner(i, offset, groups)) for i in ran...  1.9 us
  transfers between devices with their start and end apart: 9, of which 2 were waited for; matrix products, arithmetic and copies ran while one was open for 0% of the time, Pallas kernels for 33%

profile of v7, /device:TPU:1, one launch (start us, length us, event | category | flops | bytes accessed | tf_op | source)
XLA Modules:
  0.0 46.5 jit_solution(18343994798038193896)
XLA Ops:
  0.0 0.7 %convert_element_type.3.positions_ref = f32[3,32]{1,0:T(4,128)S(1)} convert(s32[3,32]{1,0:T(4,128)} %param.7) | non-fusion elementwise | flops 96 | bytes 768 | tf_op jit(solution)/shard_map/convert_element_type | solution.py:229
  0.7 0.1 pad_add_fusion.place_ref
  0.8 1.6 %copy-done = bf16[32,64,4,128]{3,2,1,0:T(4,128)(2,1)S(1)} copy-done((bf16[32,64,4,128]{3,2,1,0:T(4,128)(2,1)S(1)}, bf16[32,64,4,128]{3,2,1,0:T(4,128)(2,1)}, u32[]{:S(2)}) %copy-start) | copy-done | bytes 2097176
  2.4 2.2 %fields.2 = (bf16[4,9,32,128]{3,2,1,0:T(8,128)(2,1)S(1)}, bf16[4,9,32,128]{3,2,1,0:T(8,128)(2,1)S(1)}, bf16[4,9,32,128]{3,2,1,0:T(8,128)(2,1)S(1)}, bf16[4,9,32,...) custom-call(s32[2]{0:T(128)S(1)} %pad_add_fusion.place_ref, ...), custom_call_target="tpu_custom_call" | custom-call | tf_op jit(solution)/shard_map/fields/pallas_call | solution.py:76
  4.6 4.7 %collective-permute-start.2 = (bf16[4,9,32,128]{3,2,1,0:T(8,128)(2,1)S(1)}, bf16[4,9,32,128]{3,2,1,0:T(8,128)(2,1)S(1)}, u32[]{:S(2)}, u32[]{:S(2)}) collective-permute-start(bf16[4,9,32,128]{3,2,1,0:T(8,128)(2,1)S(1)} %get-tuple-element.29), channel_id=1, source_target_pairs={{0,48},{16,32},{32,80},{48,64},{64,112},{80,96},{96,16},{112,0},{1... | collective-permute-start | bytes 884744 | tf_op jit(solution)/shard_map/ppermute | solution.py:234
  9.2 1.4 %collective-permute-start.3 = (bf16[4,9,32,128]{3,2,1,0:T(8,128)(2,1)S(1)}, bf16[4,9,32,128]{3,2,1,0:T(8,128)(2,1)S(1)}, u32[]{:S(2)}, u32[]{:S(2)}) collective-permute-start(bf16[4,9,32,128]{3,2,1,0:T(8,128)(2,1)S(1)} %get-tuple-element.30), channel_id=1, source_target_pairs={{0,96},{16,112},{32,0},{48,16},{64,32},{80,48},{96,64},{112,80},{1... | collective-permute-start | bytes 884744 | tf_op jit(solution)/shard_map/ppermute | solution.py:234
  10.6 0.4 collective-permute-start.4
  11.0 1.5 %collective-permute-start.5 = (bf16[4,9,32,128]{3,2,1,0:T(8,128)(2,1)S(1)}, bf16[4,9,32,128]{3,2,1,0:T(8,128)(2,1)S(1)}, u32[]{:S(2)}, u32[]{:S(2)}) collective-permute-start(bf16[4,9,32,128]{3,2,1,0:T(8,128)(2,1)S(1)} %get-tuple-element.32), channel_id=1, source_target_pairs={{0,64},{16,80},{32,96},{48,112},{64,0},{80,16},{96,32},{112,48},{1... | collective-permute-start | bytes 884744 | tf_op jit(solution)/shard_map/ppermute | solution.py:234
  12.5 3.7 %collective-permute-start.6 = (bf16[4,9,32,128]{3,2,1,0:T(8,128)(2,1)S(1)}, bf16[4,9,32,128]{3,2,1,0:T(8,128)(2,1)S(1)}, u32[]{:S(2)}, u32[]{:S(2)}) collective-permute-start(bf16[4,9,32,128]{3,2,1,0:T(8,128)(2,1)S(1)} %get-tuple-element.33), channel_id=1, source_target_pairs={{0,80},{16,64},{32,112},{48,96},{64,16},{80,0},{96,48},{112,32},{1... | collective-permute-start | bytes 884744 | tf_op jit(solution)/shard_map/ppermute | solution.py:234
  16.3 10.2 %pair_weights.1 = (bf16[256,256]{1,0:T(8,128)(2,1)S(1)}, bf16[256,256]{1,0:T(8,128)(2,1)S(1)}) custom-call(s32[2]{0:T(128)S(1)} %pad_add_fusion.place_ref, s32[2,32768]{1,0:T(2,128)S(1)} %bitcast.7, f32[1,32768]{1,0:T(1,128)S(1)} %bitcast.8), custom_call_target="tpu_custom_call" | custom-call | flops 8589934592 | bytes 393216 | tf_op jit(solution)/shard_map/pair_weights/pallas_call | solution.py:117
  26.4 0.8 %fields.3.refs_0_ = bf16[4,9,32,128]{3,2,1,0:T(8,128)(2,1)S(1)} custom-call(s32[2]{0:T(128)S(1)} %pad_add_fusion.place_ref, f32[3,32]{1,0:T(4,128)S(1)} %convert_element_type.3.positions_ref, bf16[32,256,128]{2,1,0:T(8,128)(2,1)S(1)} %bitcast.6), custom_call_target="tpu_custom_call" | custom-call | tf_op jit(solution)/shard_map/fields/pallas_call | solution.py:76
  27.3 1.5 %collective-permute-start = (bf16[4,9,32,128]{3,2,1,0:T(8,128)(2,1)S(1)}, bf16[4,9,32,128]{3,2,1,0:T(8,128)(2,1)S(1)}, u32[]{:S(2)}, u32[]{:S(2)}) collective-permute-start(bf16[4,9,32,128]{3,2,1,0:T(8,128)(2,1)S(1)} %get-tuple-element.27), channel_id=1, source_target_pairs={{0,112},{16,96},{32,16},{48,0},{64,48},{80,32},{96,80},{112,64},{1... | collective-permute-start | bytes 884744 | tf_op jit(solution)/shard_map/ppermute | solution.py:234
  28.8 0.0 collective-permute-done.3.refs_2_
  28.8 0.1 collective-permute-start.1
  29.0 0.0 collective-permute-done.4.refs_3_
  29.0 1.9 %collective-permute-done.6.refs_5_ = bf16[4,9,32,128]{3,2,1,0:T(8,128)(2,1)S(1)} collective-permute-done((bf16[4,9,32,128]{3,2,1,0:T(8,128)(2,1)S(1)}, bf16[4,9,32,128]{3,2,1,0:T(8,128)(2,1)S(1)}, u32[]{:S(2)}, u32[]{:S(2)}) %collective-permute-start.6) | collective-permute-done | bytes 294944 | tf_op jit(solution)/shard_map/ppermute | solution.py:234
  30.9 3.5 %collective-permute-start.7 = (bf16[6,8,32,128]{3,2,1,0:T(8,128)(2,1)S(1)}, bf16[6,8,32,128]{3,2,1,0:T(8,128)(2,1)S(1)}, u32[]{:S(2)}, u32[]{:S(2)}) collective-permute-start(bf16[6,8,32,128]{3,2,1,0:T(8,128)(2,1)S(1)} %slice_dynamic-update-slice_fusion), channel_id=1, source_target_pairs={{1,0},{2,1},{3,2},{4,3},{5,4},{6,5},{7,6},{8,7},{9,8},{10,9},{11,1... | collective-permute-start | bytes 1179656 | tf_op jit(solution)/shard_map/ppermute | solution.py:243
  34.5 2.2 %early_slopes.1.early_ref = f32[8,4,128]{2,1,0:T(4,128)S(1)} custom-call(bf16[256,256]{1,0:T(8,128)(2,1)S(1)} %get-tuple-element.25.matrix_ref, bf16[4,9,32,128]{3,2,1,0:T(8,128)(2,1)S(1)} %fields.3.refs_0_, bf16[4,9,32,128]{3,2,1,0:T(8,128)(2,1)S(1)} %collective-permute-done.2.refs_1_, bf16[4,9,32,128]{3,2,1,0:T(8,128)(2,1)S(1)} %collective-permute-done.3.refs_2_, ...), custom_call_target="tpu_custom_call" | custom-call | flops 900000000 | bytes 3000000 | tf_op jit(solution)/shard_map/early_slopes/pallas_call | solution.py:247
  36.7 0.0 copy-start.2
  36.7 4.7 %collective-permute-start.8 = (bf16[2,8,32,128]{3,2,1,0:T(8,128)(2,1)S(1)}, bf16[2,8,32,128]{3,2,1,0:T(8,128)(2,1)S(1)}, u32[]{:S(2)}, u32[]{:S(2)}) collective-permute-start(bf16[2,8,32,128]{3,2,1,0:T(8,128)(2,1)S(1)} %pad_maximum_fusion), channel_id=1, source_target_pairs={{1,0},{2,1},{3,2},{4,3},{5,4},{6,5},{7,6},{8,7},{9,8},{10,9},{11,1... | collective-permute-start | bytes 393224 | tf_op jit(solution)/shard_map/ppermute | solution.py:243
  41.4 0.0 collective-permute-done.7.above_ref
  41.4 2.1 %late_slopes.1 = (f32[8,4,128]{2,1,0:T(4,128)S(1)}, f32[8,64,128]{2,1,0:T(8,128)S(1)}) custom-call(bf16[256,256]{1,0:T(8,128)(2,1)S(1)} %get-tuple-element.25.matrix_ref, bf16[256,256]{1,0:T(8,128)(2,1)S(1)} %get-tuple-element.26.both_ref, f32[8,4,128]{2,1,0:T(4,128)S(1)} %early_slopes.1.early_ref, ...), custom_call_target="tpu_custom_call" | custom-call | flops 700000000 | bytes 3000000 | tf_op jit(solution)/shard_map/late_slopes/pallas_call | solution.py:256
  43.6 2.0 %collective-permute-done.8.above_ref = bf16[2,8,32,128]{3,2,1,0:T(8,128)(2,1)S(1)} collective-permute-done((bf16[2,8,32,128]{3,2,1,0:T(8,128)(2,1)S(1)}, bf16[2,8,32,128]{3,2,1,0:T(8,128)(2,1)S(1)}, u32[]{:S(2)}, u32[]{:S(2)}) %collective-permute-start.8) | collective-permute-done | bytes 131104 | tf_op jit(solution)/shard_map/ppermute | solution.py:243
  45.6 0.8 %outer_slopes.1 = f32[8,4,128]{2,1,0:T(4,128)} custom-call(bf16[256,256]{1,0:T(8,128)(2,1)S(1)} %get-tuple-element.25.matrix_ref, f32[8,4,128]{2,1,0:T(4,128)S(1)} %get-tuple-element.41.inner_ref, f32[8,64,128]{2,1,0:T(8,128)S(1)} %get-tuple-element.42.mixed_ref, f32[8,4,128]{2,1,0:T(4,128)S(1)} %copy-done.2, ...), custom_call_target="tpu_custom_call" | custom-call | tf_op jit(solution)/shard_map/outer_slopes/pallas_call | solution.py:268
  (21 shorter events, 0.1 us)
Async XLA Ops:
  0.8 1.6 %copy-start = (bf16[32,64,4,128]{3,2,1,0:T(4,128)(2,1)S(1)}, bf16[32,64,4,128]{3,2,1,0:T(4,128)(2,1)}, u32[]{:S(2)}) copy-start(bf16[32,64,4,128]{3,2,1,0:T(4,128)(2,1)} %param.5) | copy-start | bytes 6291460
  2.4 13.9 %copy-start.3 = (s32[32768,2]{0,1:T(2,128)S(1)}, s32[32768,2]{0,1:T(2,128)}, u32[]{:S(2)}) copy-start(s32[32768,2]{0,1:T(2,128)} %param.8) | copy-start | bytes 786436
  2.4 13.9 %copy-start.4 = (f32[32768]{0:T(1024)S(1)}, f32[32768]{0:T(1024)}, u32[]{:S(2)}) copy-start(f32[32768]{0:T(1024)} %param.9) | copy-start | bytes 393220
  4.6 22.7 %collective-permute-start.2 = (bf16[4,9,32,128]{3,2,1,0:T(8,128)(2,1)S(1)}, bf16[4,9,32,128]{3,2,1,0:T(8,128)(2,1)S(1)}, u32[]{:S(2)}, u32[]{:S(2)}) collective-permute-start(bf16[4,9,32,128]{3,2,1,0:T(8,128)(2,1)S(1)} %get-tuple-element.29), channel_id=1, source_target_pairs={{0,48},{16,32},{32,80},{48,64},{64,112},{80,96},{96,16},{112,0},{1... | collective-permute-start | bytes 884744 | tf_op jit(solution)/shard_map/ppermute | solution.py:234
  9.2 19.6 %collective-permute-start.3 = (bf16[4,9,32,128]{3,2,1,0:T(8,128)(2,1)S(1)}, bf16[4,9,32,128]{3,2,1,0:T(8,128)(2,1)S(1)}, u32[]{:S(2)}, u32[]{:S(2)}) collective-permute-start(bf16[4,9,32,128]{3,2,1,0:T(8,128)(2,1)S(1)} %get-tuple-element.30), channel_id=1, source_target_pairs={{0,96},{16,112},{32,0},{48,16},{64,32},{80,48},{96,64},{112,80},{1... | collective-permute-start | bytes 884744 | tf_op jit(solution)/shard_map/ppermute | solution.py:234
  10.6 18.3 %collective-permute-start.4 = (bf16[4,9,32,128]{3,2,1,0:T(8,128)(2,1)S(1)}, bf16[4,9,32,128]{3,2,1,0:T(8,128)(2,1)S(1)}, u32[]{:S(2)}, u32[]{:S(2)}) collective-permute-start(bf16[4,9,32,128]{3,2,1,0:T(8,128)(2,1)S(1)} %get-tuple-element.31), channel_id=1, source_target_pairs={{0,16},{16,0},{32,48},{48,32},{64,80},{80,64},{96,112},{112,96},{1... | collective-permute-start | bytes 884744 | tf_op jit(solution)/shard_map/ppermute | solution.py:234
  11.0 17.9 %collective-permute-start.5 = (bf16[4,9,32,128]{3,2,1,0:T(8,128)(2,1)S(1)}, bf16[4,9,32,128]{3,2,1,0:T(8,128)(2,1)S(1)}, u32[]{:S(2)}, u32[]{:S(2)}) collective-permute-start(bf16[4,9,32,128]{3,2,1,0:T(8,128)(2,1)S(1)} %get-tuple-element.32), channel_id=1, source_target_pairs={{0,64},{16,80},{32,96},{48,112},{64,0},{80,16},{96,32},{112,48},{1... | collective-permute-start | bytes 884744 | tf_op jit(solution)/shard_map/ppermute | solution.py:234
  12.5 18.3 %collective-permute-start.6 = (bf16[4,9,32,128]{3,2,1,0:T(8,128)(2,1)S(1)}, bf16[4,9,32,128]{3,2,1,0:T(8,128)(2,1)S(1)}, u32[]{:S(2)}, u32[]{:S(2)}) collective-permute-start(bf16[4,9,32,128]{3,2,1,0:T(8,128)(2,1)S(1)} %get-tuple-element.33), channel_id=1, source_target_pairs={{0,80},{16,64},{32,112},{48,96},{64,16},{80,0},{96,48},{112,32},{1... | collective-permute-start | bytes 884744 | tf_op jit(solution)/shard_map/ppermute | solution.py:234
  16.3 10.2 %copy-start.1 = (bf16[32,64,4,128]{3,2,1,0:T(4,128)(2,1)S(1)}, bf16[32,64,4,128]{3,2,1,0:T(4,128)(2,1)}, u32[]{:S(2)}) copy-start(bf16[32,64,4,128]{3,2,1,0:T(4,128)(2,1)} %param.5) | copy-start | bytes 6291460
  27.3 9.4 %collective-permute-start = (bf16[4,9,32,128]{3,2,1,0:T(8,128)(2,1)S(1)}, bf16[4,9,32,128]{3,2,1,0:T(8,128)(2,1)S(1)}, u32[]{:S(2)}, u32[]{:S(2)}) collective-permute-start(bf16[4,9,32,128]{3,2,1,0:T(8,128)(2,1)S(1)} %get-tuple-element.27), channel_id=1, source_target_pairs={{0,112},{16,96},{32,16},{48,0},{64,48},{80,32},{96,80},{112,64},{1... | collective-permute-start | bytes 884744 | tf_op jit(solution)/shard_map/ppermute | solution.py:234
  28.8 7.9 %collective-permute-start.1 = (bf16[4,9,32,128]{3,2,1,0:T(8,128)(2,1)S(1)}, bf16[4,9,32,128]{3,2,1,0:T(8,128)(2,1)S(1)}, u32[]{:S(2)}, u32[]{:S(2)}) collective-permute-start(bf16[4,9,32,128]{3,2,1,0:T(8,128)(2,1)S(1)} %get-tuple-element.28), channel_id=1, source_target_pairs={{0,32},{16,48},{32,64},{48,80},{64,96},{80,112},{96,0},{112,16},{1... | collective-permute-start | bytes 884744 | tf_op jit(solution)/shard_map/ppermute | solution.py:234
  30.9 10.5 %collective-permute-start.7 = (bf16[6,8,32,128]{3,2,1,0:T(8,128)(2,1)S(1)}, bf16[6,8,32,128]{3,2,1,0:T(8,128)(2,1)S(1)}, u32[]{:S(2)}, u32[]{:S(2)}) collective-permute-start(bf16[6,8,32,128]{3,2,1,0:T(8,128)(2,1)S(1)} %slice_dynamic-update-slice_fusion), channel_id=1, source_target_pairs={{1,0},{2,1},{3,2},{4,3},{5,4},{6,5},{7,6},{8,7},{9,8},{10,9},{11,1... | collective-permute-start | bytes 1179656 | tf_op jit(solution)/shard_map/ppermute | solution.py:243
  36.7 9.0 %copy-start.2 = (f32[8,4,128]{2,1,0:T(4,128)S(1)}, f32[8,4,128]{2,1,0:T(4,128)}, u32[]{:S(2)}) copy-start(f32[8,4,128]{2,1,0:T(4,128)} %conductivity_ref.1) | copy-start | bytes 49156
  36.7 8.9 %collective-permute-start.8 = (bf16[2,8,32,128]{3,2,1,0:T(8,128)(2,1)S(1)}, bf16[2,8,32,128]{3,2,1,0:T(8,128)(2,1)S(1)}, u32[]{:S(2)}, u32[]{:S(2)}) collective-permute-start(bf16[2,8,32,128]{3,2,1,0:T(8,128)(2,1)S(1)} %pad_maximum_fusion), channel_id=1, source_target_pairs={{1,0},{2,1},{3,2},{4,3},{5,4},{6,5},{7,6},{8,7},{9,8},{10,9},{11,1... | collective-permute-start | bytes 393224 | tf_op jit(solution)/shard_map/ppermute | solution.py:243
